TPU v7x, 32 devices: a whole 2x2x4 slice. The times are simulated.
32 devices in a mesh: section: 2 (over core), dp: 16 (over z, y, x).
Axes of the slice: x: 2, y: 2, z: 4, core: 2. Of those that a mesh axis runs over, the one named last changes fastest.
Arguments:
- inputs: bfloat16 [2, 3072, 1024], P(None, 'dp', 'section'), may hold values from -6 to 6
- lengths: int32 [2, 16, 5], P(None, 'dp'), may hold values from 1 to 64, 128 in all within a row
- labels: int32 [2, 32], replicated, may hold values from 0 to 63, as said below
- w_qkv: float32 [2, 1024, 3072], P('section', 'dp'), may hold values from -0.1875 to 0.1875
- w_out: float32 [2, 1024, 1024], P('section', 'dp'), may hold values from -0.5 to 0.5
- w_up: float32 [2, 1024, 4096], P('section', 'dp'), may hold values from -0.1875 to 0.1875
- w_down: float32 [2, 4096, 1024], P('section', 'dp'), may hold values from -0.125 to 0.125
- ln_gain: float32 [2, 2, 1024], P('section', None, 'dp'), may hold values from 0.5 to 1.5
- ln_bias: float32 [2, 2, 1024], P('section', None, 'dp'), may hold values from -2 to 2
- head_a: float32 [1024, 128], P(('section', 'dp')), may hold values from -0.1875 to 0.1875
- head_b: float32 [1024, 96], P(('section', 'dp')), may hold values from -0.1875 to 0.1875
- head_c: float32 [1024, 64], P(('section', 'dp')), may hold values from -0.1875 to 0.1875
Outputs:
- loss: float32 [2, 16, 2], P(None, 'dp', 'section')
- grad_inputs: float32 [2, 3072, 1024], P(None, 'dp', 'section')
- grad_qkv: float32 [2, 1024, 3072], P('section', 'dp')
- grad_out: float32 [2, 1024, 1024], P('section', 'dp')
- grad_up: float32 [2, 1024, 4096], P('section', 'dp')
- grad_down: float32 [2, 4096, 1024], P('section', 'dp')
- grad_gain: float32 [2, 2, 1024], P('section', None, 'dp')
- grad_bias: float32 [2, 2, 1024], P('section', None, 'dp')
- grad_head_a: float32 [1024, 128], P(('section', 'dp'))
- grad_head_b: float32 [1024, 96], P(('section', 'dp'))
- grad_head_c: float32 [1024, 64], P(('section', 'dp'))
Inputs may be any that keep to these rules, and one draw needn't show every extreme that they name: Each row's 4 document lengths and its final pad length sum to 128; every entry is at least 1. `labels`: global document numbers of the same micro-batch.
All inputs are finite; a program needn't handle non-finite values.
Results may differ from a plain program's by a relative error of at most 0.017.
The roundings to bfloat16 on the way count: a program that leaves them out, or rounds other values in their place, can miss the bound.
Values may be sent and summed in bfloat16 or wider, within the bound.
No kernel may reach another device: no remote copies, remote signals or barrier semaphores. Data moves between devices by JAX's collectives and lax.ppermute only.
A program may use at most 192 MiB of HBM per device.

v0:
```python
import math

import jax
import jax.numpy as jnp
from jax import lax
from jax.sharding import PartitionSpec as P

D = 1024
HEADS = 16
DH = 64
ROW = 128
NSEG = 4
QDEV = 2
QLEN = 32


ln_eps = 1e-05
norm_eps = 1e-06
sharpness = 16.0
masked_score = -1000000000.0
highest = lax.Precision.HIGHEST


def cut_along(array, dim, peers):
    before, after = (array.shape[:dim], array.shape[dim + 1 :])
    return jnp.moveaxis(array.reshape(*before, peers, -1, *after), dim, 0)


def sum_at_owner(array, axis, dim):
    tiles = cut_along(array, dim, lax.axis_size(axis))
    arrived = lax.all_to_all(tiles, axis, split_axis=0, concat_axis=0, tiled=True)
    return arrived.astype(jnp.float32).sum(axis=0)


def side_by_side(arrays, axis, dim, along):
    widths = [a.shape[along] for a in arrays]
    both = jnp.concatenate(arrays, axis=along)
    out = sum_at_owner(both, axis, dim)
    return tuple(jnp.split(out, [sum(widths[:k]) for k in range(1, len(widths))], axis=along))


def from_behind(value, axis, steps):
    count = lax.axis_size(axis)
    leading, last = (max(0, -steps), min(count, count - steps))
    return lax.ppermute(value, axis, [(source, source + steps) for source in range(leading, last)])


def layout(row_lengths):
    ends = jnp.cumsum(row_lengths)
    starts = ends - row_lengths
    places = jnp.arange(ROW, dtype=jnp.int32)
    doc_seg = jnp.sum((places[:, None] >= ends[None, :]).astype(jnp.int32), axis=1)
    owners = doc_seg[:, None] == jnp.arange(NSEG + 1, dtype=jnp.int32)[None, :]
    doc_pos = places - jnp.sum(jnp.where(owners, starts[None, :], 0), axis=1)
    query_places = jnp.arange(QDEV * QLEN, dtype=jnp.int32)
    query_seg = NSEG + 1 + query_places // QLEN
    query_pos = query_places % QLEN
    segment_ids = jnp.concatenate([doc_seg, query_seg])
    positions = jnp.concatenate([doc_pos, query_pos])
    return (segment_ids, positions)


def rotary(positions):
    half_dim = DH // 2
    freqs = jnp.exp(jnp.arange(half_dim, dtype=jnp.float32) * (-math.log(10000.0) / half_dim))
    angles = positions.astype(jnp.float32)[..., None] * freqs
    cosine = jnp.cos(angles)
    sine = jnp.sin(angles)
    return (jnp.concatenate([cosine, cosine], -1), jnp.concatenate([sine, sine], -1))


def rope(values, cosine, sine):
    half_dim = values.shape[-1] // 2
    turned = jnp.concatenate([-values[..., half_dim:], values[..., :half_dim]], -1)
    return values * cosine[..., None, :] + turned * sine[..., None, :]


def layer_norm(values, gain, bias):
    centre = values - jnp.mean(values, -1, keepdims=True)
    variance = jnp.mean(centre * centre, -1, keepdims=True)
    return centre * lax.rsqrt(variance + ln_eps) * gain + bias


def gelu_exact(values):
    return jax.nn.gelu(values, approximate=False)


def unit_rows(values):
    return values * lax.rsqrt(jnp.sum(values * values, -1, keepdims=True) + norm_eps)


def dot_plain(left, right):
    return jnp.dot(left, right, preferred_element_type=jnp.float32)


def dot_left_t(left, right):
    return lax.dot_general(
        left, right, (((0,), (0,)), ((), ())), preferred_element_type=jnp.float32
    )


def dot_right_t(left, right):
    return lax.dot_general(
        left, right, (((1,), (1,)), ((), ())), preferred_element_type=jnp.float32
    )


def split_heads(values):
    return values.reshape(values.shape[0], HEADS, DH)


def masked_scores(q_rot, k_rot, segments):
    scores = jnp.einsum("thd,uhd->htu", q_rot, k_rot, preferred_element_type=jnp.float32) * 0.125
    same_doc = segments[:, None] == segments[None, :]
    return jnp.where(same_doc[None], scores, masked_score)


def layer_forward(entry, weights, segments, cosine, sine):
    w_qkv, w_out, w_up, w_down, gains, biases = weights
    tok_rows = entry.shape[0]
    mixed_in = dot_plain(entry, w_qkv)
    q_rot = rope(split_heads(mixed_in[:, :D]), cosine, sine).astype(jnp.bfloat16)
    k_rot = rope(split_heads(mixed_in[:, D : 2 * D]), cosine, sine).astype(jnp.bfloat16)
    v_low = split_heads(mixed_in[:, 2 * D :]).astype(jnp.bfloat16)
    scores = masked_scores(q_rot, k_rot, segments)
    peak_score = jnp.max(scores, -1, keepdims=True)
    raised_exp = jnp.exp(scores - peak_score)
    row_total = jnp.sum(raised_exp, -1, keepdims=True)
    weights_soft = raised_exp / row_total
    log_total = peak_score + jnp.log(row_total)
    attended = jnp.einsum(
        "htu,uhd->thd", weights_soft.astype(jnp.bfloat16), v_low, preferred_element_type=jnp.float32
    )
    o_low = attended.reshape(tok_rows, D).astype(jnp.bfloat16)
    branch = dot_plain(o_low, w_out)
    middle = layer_norm(entry.astype(jnp.float32) + branch, gains[0], biases[0])
    raised = dot_plain(middle.astype(jnp.bfloat16), w_up)
    active = gelu_exact(raised).astype(jnp.bfloat16)
    lowered = dot_plain(active, w_down)
    result = layer_norm(middle + lowered, gains[1], biases[1])
    kept = (entry, q_rot, k_rot, v_low, log_total, o_low, branch, middle, raised, active, lowered)
    return (result, kept)


def layer_backward(grad_out, kept, weights, segments, cosine, sine):
    entry, q_rot, k_rot, v_low, log_total, o_low, branch, middle, raised, active, lowered = kept
    w_qkv, w_out, w_up, w_down, gains, biases = weights
    tok_rows = entry.shape[0]
    _, pull_two = jax.vjp(layer_norm, middle + lowered, gains[1], biases[1])
    d_two, d_gain_two, d_bias_two = pull_two(grad_out)
    d_lowered = d_two.astype(jnp.bfloat16)
    d_active = dot_right_t(d_lowered, w_down)
    g_down = dot_left_t(active, d_lowered)
    _, pull_gelu = jax.vjp(gelu_exact, raised)
    d_raised = pull_gelu(d_active)[0].astype(jnp.bfloat16)
    g_up = dot_left_t(middle.astype(jnp.bfloat16), d_raised)
    d_middle = d_two + dot_right_t(d_raised, w_up)
    _, pull_one = jax.vjp(layer_norm, entry.astype(jnp.float32) + branch, gains[0], biases[0])
    d_one, d_gain_one, d_bias_one = pull_one(d_middle)
    d_branch = d_one.astype(jnp.bfloat16)
    g_out = dot_left_t(o_low, d_branch)
    d_attended = split_heads(dot_right_t(d_branch, w_out).astype(jnp.bfloat16))
    scores = masked_scores(q_rot, k_rot, segments)
    weights_soft = jnp.exp(scores - log_total)
    d_weights = jnp.einsum("thd,uhd->htu", d_attended, v_low, preferred_element_type=jnp.float32)
    g_value = jnp.einsum(
        "htu,thd->uhd",
        weights_soft.astype(jnp.bfloat16),
        d_attended,
        preferred_element_type=jnp.float32,
    )
    inner = jnp.sum(weights_soft * d_weights, -1, keepdims=True)
    d_scores = (weights_soft * (d_weights - inner)).astype(jnp.bfloat16)
    d_qrot = jnp.einsum("htu,uhd->thd", d_scores, k_rot, preferred_element_type=jnp.float32) * 0.125
    d_krot = jnp.einsum("htu,thd->uhd", d_scores, q_rot, preferred_element_type=jnp.float32) * 0.125
    _, rope_pull = jax.vjp(lambda rotated: rope(rotated, cosine, sine), d_qrot)
    d_query = rope_pull(d_qrot)[0]
    d_key = rope_pull(d_krot)[0]
    d_mixed = jnp.concatenate(
        [d_query.reshape(tok_rows, D), d_key.reshape(tok_rows, D), g_value.reshape(tok_rows, D)],
        axis=1,
    ).astype(jnp.bfloat16)
    g_qkv = dot_left_t(entry, d_mixed)
    d_entry = d_one + dot_right_t(d_mixed, w_qkv)
    grads = (
        g_qkv,
        g_out,
        g_up,
        g_down,
        jnp.stack([d_gain_one, d_gain_two]),
        jnp.stack([d_bias_one, d_bias_two]),
    )
    return (d_entry, grads)


def head_pass(final, heads, segments, labels_row, dp_index):
    flat_rows = final.astype(jnp.bfloat16)
    member = (segments[:ROW, None] == jnp.arange(NSEG, dtype=jnp.int32)[None, :]).astype(
        jnp.float32
    )
    embedded = [dot_plain(flat_rows, w_head) for w_head in heads]
    unit_list = [unit_rows(item).astype(jnp.bfloat16) for item in embedded]
    all_queries = (
        lax.all_gather(unit_list[0][ROW:], "dp", axis=0, tiled=True),
        lax.all_gather(unit_list[1][ROW:], "dp", axis=0, tiled=True),
        lax.all_gather(unit_list[2][ROW:], "dp", axis=0, tiled=True),
    )
    exponents = []
    masses = []
    local_logits = []
    for head_idx in range(3):
        similar = dot_right_t(all_queries[head_idx], unit_list[head_idx][:ROW])
        expo_sim = jnp.exp(sharpness * similar)
        mass_sum = jnp.dot(expo_sim, member, precision=highest, preferred_element_type=jnp.float32)
        token_score = jnp.log(mass_sum) / sharpness
        exponents.append(expo_sim)
        masses.append(mass_sum)
        local_logits.append(jnp.sum(token_score.reshape(-1, QLEN, NSEG), axis=1))
    logits = lax.all_gather(jnp.stack(local_logits), "dp", axis=2, tiled=True)
    doc_count = logits.shape[2]
    label_hot = (jnp.arange(doc_count, dtype=jnp.int32)[None, :] == labels_row[:, None]).astype(
        jnp.float32
    )
    peak_logit = jnp.max(logits, -1, keepdims=True)
    spread = jnp.exp(logits - peak_logit)
    totals = jnp.sum(spread, -1, keepdims=True)
    per_query = jnp.sum(
        peak_logit[..., 0] + jnp.log(totals[..., 0]) - jnp.sum(logits * label_hot[None], -1), axis=0
    )
    own_losses = lax.dynamic_slice_in_dim(per_query, dp_index * QDEV, QDEV)
    d_logits = spread / totals - label_hot[None]
    d_local = lax.dynamic_slice_in_dim(d_logits, dp_index * NSEG, NSEG, 2)
    d_query_list = []
    d_doc_list = []
    for head_idx in range(3):
        d_token = jnp.repeat(d_local[head_idx], QLEN, axis=0)
        d_mass = d_token / (sharpness * masses[head_idx])
        d_expo = jnp.dot(d_mass, member.T, precision=highest, preferred_element_type=jnp.float32)
        d_similar = (d_expo * exponents[head_idx] * sharpness).astype(jnp.bfloat16)
        d_query_list.append(dot_plain(d_similar, unit_list[head_idx][:ROW]))
        d_doc_list.append(dot_left_t(d_similar, all_queries[head_idx]))
    query_back = side_by_side(
        (
            d_query_list[0].astype(jnp.bfloat16),
            d_query_list[1].astype(jnp.bfloat16),
            d_query_list[2].astype(jnp.bfloat16),
        ),
        "dp",
        0,
        1,
    )
    d_final = jnp.zeros(final.shape, jnp.float32)
    head_grads = []
    for head_idx in range(3):
        d_unit = jnp.concatenate([d_doc_list[head_idx], query_back[head_idx]], axis=0)
        _, norm_pull = jax.vjp(unit_rows, embedded[head_idx])
        d_embedded = norm_pull(d_unit)[0].astype(jnp.bfloat16)
        head_grads.append(dot_left_t(flat_rows, d_embedded))
        d_final = d_final + dot_right_t(d_embedded, heads[head_idx])
    return (own_losses, d_final, head_grads)


def on_device(
    inputs, lengths, labels, w_qkv, w_out, w_up, w_down, ln_gain, ln_bias, head_a, head_b, head_c
):
    micro = inputs.shape[0]
    section_index = lax.axis_index("section")
    dp_index = lax.axis_index("dp")
    is_first = section_index == 0
    other_half = from_behind(inputs, "section", -1)
    whole_inputs = jnp.concatenate([inputs, other_half], axis=2)
    gathered = (
        lax.all_gather(w_qkv.astype(jnp.bfloat16), "dp", axis=1, tiled=True),
        lax.all_gather(w_out.astype(jnp.bfloat16), "dp", axis=1, tiled=True),
        lax.all_gather(w_up.astype(jnp.bfloat16), "dp", axis=1, tiled=True),
        lax.all_gather(w_down.astype(jnp.bfloat16), "dp", axis=1, tiled=True),
        lax.all_gather(ln_gain.astype(jnp.bfloat16), "dp", axis=2, tiled=True),
        lax.all_gather(ln_bias.astype(jnp.bfloat16), "dp", axis=2, tiled=True),
    )
    weights = (
        gathered[0][0],
        gathered[1][0],
        gathered[2][0],
        gathered[3][0],
        gathered[4][0].astype(jnp.float32),
        gathered[5][0].astype(jnp.float32),
    )
    heads = (
        lax.all_gather(head_a.astype(jnp.bfloat16), ("section", "dp"), axis=0, tiled=True),
        lax.all_gather(head_b.astype(jnp.bfloat16), ("section", "dp"), axis=0, tiled=True),
        lax.all_gather(head_c.astype(jnp.bfloat16), ("section", "dp"), axis=0, tiled=True),
    )
    seg_list = []
    cos_list = []
    sin_list = []
    for micro_idx in range(micro):
        segment_ids, positions = layout(lengths[micro_idx, 0])
        cosine, sine = rotary(positions)
        seg_list.append(segment_ids)
        cos_list.append(cosine)
        sin_list.append(sine)
    tok_rows = whole_inputs.shape[1]
    received = jnp.zeros((tok_rows, D), jnp.bfloat16)
    kept_list = []
    finals = []
    for tick_idx in range(micro + 1):
        own_idx = min(tick_idx, micro - 1)
        prior_idx = max(tick_idx - 1, 0)
        segments = jnp.where(is_first, seg_list[own_idx], seg_list[prior_idx])
        cosine = jnp.where(is_first, cos_list[own_idx], cos_list[prior_idx])
        sine = jnp.where(is_first, sin_list[own_idx], sin_list[prior_idx])
        entry = jnp.where(is_first, whole_inputs[own_idx], received)
        result, kept = layer_forward(entry, weights, segments, cosine, sine)
        kept_list.append(kept)
        if tick_idx >= 1:
            finals.append(result)
        if tick_idx < micro:
            received = from_behind(result.astype(jnp.bfloat16), "section", 1)
    losses = []
    d_finals = []
    head_sums = [jnp.zeros(item.shape, jnp.float32) for item in heads]
    for micro_idx in range(micro):
        own_losses, d_final, head_grads = head_pass(
            finals[micro_idx], heads, seg_list[micro_idx], labels[micro_idx], dp_index
        )
        losses.append(own_losses)
        d_finals.append(d_final)
        head_sums = [total_sum + grad_item for total_sum, grad_item in zip(head_sums, head_grads)]
    last_mask = jnp.where(is_first, 0.0, 1.0)
    head_sums = [total_sum * last_mask for total_sum in head_sums]
    received_grad = jnp.zeros((tok_rows, D), jnp.bfloat16)
    grad_shards = None
    grad_totals = None
    input_grads = []
    for tick_idx in range(micro + 1):
        own_idx = min(tick_idx, micro - 1)
        prior_idx = max(tick_idx - 1, 0)
        later_idx = min(tick_idx + 1, micro)
        kept = jax.tree.map(
            lambda early_item, late_item: jnp.where(is_first, early_item, late_item),
            kept_list[prior_idx],
            kept_list[later_idx],
        )
        segments = jnp.where(is_first, seg_list[prior_idx], seg_list[own_idx])
        cosine = jnp.where(is_first, cos_list[prior_idx], cos_list[own_idx])
        sine = jnp.where(is_first, sin_list[prior_idx], sin_list[own_idx])
        grad_in = jnp.where(is_first, received_grad.astype(jnp.float32), d_finals[own_idx])
        d_entry, grads = layer_backward(grad_in, kept, weights, segments, cosine, sine)
        valid = jnp.where(is_first, float(tick_idx >= 1), float(tick_idx < micro))
        grads = tuple((grad_item * valid for grad_item in grads))
        grad_totals = (
            grads
            if grad_totals is None
            else tuple((acc + item for acc, item in zip(grad_totals, grads)))
        )
        if tick_idx >= 1:
            input_grads.append(d_entry)
        if tick_idx < micro:
            received_grad = from_behind(d_entry.astype(jnp.bfloat16), "section", -1)
    grad_shards = (
        lax.psum_scatter(grad_totals[0], "dp", scatter_dimension=0, tiled=True),
        lax.psum_scatter(grad_totals[1], "dp", scatter_dimension=0, tiled=True),
        lax.psum_scatter(grad_totals[2], "dp", scatter_dimension=0, tiled=True),
        lax.psum_scatter(grad_totals[3], "dp", scatter_dimension=0, tiled=True),
        lax.psum_scatter(grad_totals[4], "dp", scatter_dimension=1, tiled=True),
        lax.psum_scatter(grad_totals[5], "dp", scatter_dimension=1, tiled=True),
    )
    head_shards = (
        lax.psum_scatter(head_sums[0], ("section", "dp"), scatter_dimension=0, tiled=True),
        lax.psum_scatter(head_sums[1], ("section", "dp"), scatter_dimension=0, tiled=True),
        lax.psum_scatter(head_sums[2], ("section", "dp"), scatter_dimension=0, tiled=True),
    )
    half_width = D // 2
    input_all = jnp.stack(input_grads)
    upper_part = from_behind(
        input_all[:, :, half_width:].astype(jnp.bfloat16), "section", 1
    ).astype(jnp.float32)
    grad_inputs = jnp.where(is_first, input_all[:, :, :half_width], upper_part)
    half_queries = QDEV // 2
    loss_all = jnp.stack(losses)
    lower_part = from_behind(loss_all[:, :half_queries], "section", -1)
    loss_out = jnp.where(is_first, lower_part, loss_all[:, half_queries:])[:, None, :]
    return (
        loss_out,
        grad_inputs,
        grad_shards[0][None],
        grad_shards[1][None],
        grad_shards[2][None],
        grad_shards[3][None],
        grad_shards[4][None],
        grad_shards[5][None],
        head_shards[0],
        head_shards[1],
        head_shards[2],
    )


def solution(mesh):
    placed = (
        P(None, "dp", "section"),
        P(None, "dp", None),
        P(),
        P("section", "dp", None),
        P("section", "dp", None),
        P("section", "dp", None),
        P("section", "dp", None),
        P("section", None, "dp"),
        P("section", None, "dp"),
        P(("section", "dp"), None),
        P(("section", "dp"), None),
        P(("section", "dp"), None),
    )
    return jax.shard_map(
        on_device,
        mesh=mesh,
        in_specs=placed,
        out_specs=(
            P(None, "dp", "section"),
            P(None, "dp", "section"),
            P("section", "dp", None),
            P("section", "dp", None),
            P("section", "dp", None),
            P("section", "dp", None),
            P("section", None, "dp"),
            P("section", None, "dp"),
            P(("section", "dp"), None),
            P(("section", "dp"), None),
            P(("section", "dp"), None),
        ),
        check_vma=False,
    )
```

profile of v0, /device:TPU:10, one launch (start us, length us, event | category | flops | bytes accessed | tf_op | source)
XLA Modules:
  0.0 2788.3 jit_solution(4752936398927879211)
XLA Ops:
  16.0 36.2 %all_gather.53 = bf16[1,2,1024]{1,0,2:T(2,128)(2,1)S(1)} all-gather(bf16[1,2,64]{1,0,2:T(2,128)(2,1)S(1)} %copy.220), channel_id=1, replica_groups=mesh['section'=2,'dp'=16] {'dp'}, dimensions={2}, use_global_device_ids=true | all-gather | bytes 4352 | tf_op jit(solution)/shard_map/all_gather | solution.py:277
  57.1 6.2 slice_reduce_fusion.1
  63.3 78.1 %all_gather.59 = bf16[1024,96]{1,0:T(8,128)(2,1)} all-gather(bf16[32,96]{1,0:T(8,128)(2,1)S(1)} %convert_element_type.387), channel_id=1, replica_groups=mesh['section'=2,'dp'=16] {'section','dp'}, dimensions={0}, use_global_device_ids=true | all-gather | bytes 202752 | tf_op jit(solution)/shard_map/all_gather | solution.py:290
  141.6 39.4 %all_gather.54 = bf16[1,2,1024]{1,0,2:T(2,128)(2,1)S(1)} all-gather(bf16[1,2,64]{1,0,2:T(2,128)(2,1)S(1)} %copy.221), channel_id=1, replica_groups=mesh['section'=2,'dp'=16] {'dp'}, dimensions={2}, use_global_device_ids=true | all-gather | bytes 4352 | tf_op jit(solution)/shard_map/all_gather | solution.py:278
  182.3 6.2 slice_reduce_fusion
  188.6 4.8 fusion.34
  208.4 85.1 %all-gather.9.cloned.1.call-done = bf16[1,1024,4096]{2,1,0:T(8,128)(2,1)} async-done(((bf16[1,64,4096]{2,1,0:T(8,128)(2,1)}), bf16[1,1024,4096]{2,1,0:T(8,128)(2,1)}) %all-gather.9.cloned.1.call-update) | async-done | bytes 8388624 | tf_op jit(solution)/shard_map/all_gather | solution.py:275
  293.5 12.2 fusion.38
  305.7 102.0 %all-gather.11.cloned.1.call-done = bf16[1,4096,1024]{2,1,0:T(8,128)(2,1)} async-done(((bf16[1,256,1024]{2,1,0:T(8,128)(2,1)}), bf16[1,4096,1024]{2,1,0:T(8,128)(2,1)}) %all-gather.11.cloned.1.call-update) | async-done | bytes 8388624 | tf_op jit(solution)/shard_map/all_gather | solution.py:276
  407.8 6.7 fusion.362
  416.3 67.2 %all_gather.61 = bf16[1024,64]{1,0:T(8,128)(2,1)} all-gather(bf16[32,64]{1,0:T(8,128)(2,1)S(1)} %convert_element_type.389), channel_id=1, replica_groups=mesh['section'=2,'dp'=16] {'section','dp'}, dimensions={0}, use_global_device_ids=true | all-gather | bytes 135168 | tf_op jit(solution)/shard_map/all_gather | solution.py:291
  483.5 71.5 %all_gather.57 = bf16[1024,128]{1,0:T(8,128)(2,1)} all-gather(bf16[32,128]{1,0:T(8,128)(2,1)S(1)} %convert_element_type.385), channel_id=1, replica_groups=mesh['section'=2,'dp'=16] {'section','dp'}, dimensions={0}, use_global_device_ids=true | all-gather | bytes 270336 | tf_op jit(solution)/shard_map/all_gather | solution.py:289
  570.0 9.5 fusion.41
  594.1 39.0 %all_gather.60 = bf16[1024,96]{1,0:T(8,128)(2,1)} all-gather(bf16[64,96]{1,0:T(8,128)(2,1)} %copy.226), channel_id=1, replica_groups=mesh['section'=2,'dp'=16] {'dp'}, dimensions={0}, use_global_device_ids=true | all-gather | bytes 208896 | tf_op jit(solution)/shard_map/all_gather | solution.py:205
  633.1 41.6 %all_gather.58 = bf16[1024,128]{1,0:T(8,128)(2,1)} all-gather(bf16[64,128]{1,0:T(8,128)(2,1)} %slice.261), channel_id=1, replica_groups=mesh['section'=2,'dp'=16] {'dp'}, dimensions={0}, use_global_device_ids=true | all-gather | bytes 278528 | tf_op jit(solution)/shard_map/all_gather | solution.py:204
  674.7 37.6 %all_gather.62 = bf16[1024,64]{1,0:T(8,128)(2,1)S(1)} all-gather(bf16[64,64]{1,0:T(8,128)(2,1)} %copy.227), channel_id=1, replica_groups=mesh['section'=2,'dp'=16] {'dp'}, dimensions={0}, use_global_device_ids=true | all-gather | bytes 139264 | tf_op jit(solution)/shard_map/all_gather | solution.py:206
  732.6 38.1 %all_gather.63 = f32[3,32,64]{1,0,2:T(4,128)S(1)} all-gather(f32[3,32,4]{1,0,2:T(4,128)S(1)} %copy.228), channel_id=1, replica_groups=mesh['section'=2,'dp'=16] {'dp'}, dimensions={2}, use_global_device_ids=true | all-gather | bytes 26112 | tf_op jit(solution)/shard_map/all_gather | solution.py:219
  797.0 10.4 all-to-all-start
  812.3 4.3 fusion.30
  837.5 9.8 fusion.44
  882.0 33.7 %all_gather.65 = bf16[1024,96]{1,0:T(8,128)(2,1)} all-gather(bf16[64,96]{1,0:T(8,128)(2,1)} %copy.233), channel_id=1, replica_groups=mesh['section'=2,'dp'=16] {'dp'}, dimensions={0}, use_global_device_ids=true | all-gather | bytes 208896 | tf_op jit(solution)/shard_map/all_gather | solution.py:205
  915.7 44.4 %all_gather.64 = bf16[1024,128]{1,0:T(8,128)(2,1)} all-gather(bf16[64,128]{1,0:T(8,128)(2,1)} %slice.274), channel_id=1, replica_groups=mesh['section'=2,'dp'=16] {'dp'}, dimensions={0}, use_global_device_ids=true | all-gather | bytes 278528 | tf_op jit(solution)/shard_map/all_gather | solution.py:204
  960.1 37.3 %all_gather.66 = bf16[1024,64]{1,0:T(8,128)(2,1)S(1)} all-gather(bf16[64,64]{1,0:T(8,128)(2,1)} %copy.234), channel_id=1, replica_groups=mesh['section'=2,'dp'=16] {'dp'}, dimensions={0}, use_global_device_ids=true | all-gather | bytes 139264 | tf_op jit(solution)/shard_map/all_gather | solution.py:206
  1016.9 38.7 %all_gather.67 = f32[3,32,64]{1,0,2:T(4,128)S(1)} all-gather(f32[3,32,4]{1,0,2:T(4,128)S(1)} %copy.235), channel_id=1, replica_groups=mesh['section'=2,'dp'=16] {'dp'}, dimensions={2}, use_global_device_ids=true | all-gather | bytes 26112 | tf_op jit(solution)/shard_map/all_gather | solution.py:219
  1080.1 10.1 all-to-all-start.1
  1090.3 13.1 fusion.49
  1103.5 7.7 multiply_reduce_fusion.8
  1148.4 12.4 fusion.54
  1185.3 11.8 fusion.59
  1197.3 4.5 multiply_reduce_fusion.4
  1221.9 6.4 multiply_add_fusion.3
  1229.4 8.1 fusion.220
  1237.5 6.5 fusion.219
  1253.8 13.8 multiply_add_fusion.2
  1269.0 9.8 fusion.234
  1278.7 8.2 fusion.232
  1287.0 18.9 multiply_add_fusion.1
  1306.5 10.0 fusion.123
  1316.6 8.2 fusion.121
  1324.8 19.9 multiply_add_fusion
  1346.0 5.3 fusion.159
  1360.5 122.5 %reduce-scatter.26.cloned.1.call-done = f32[32,64]{1,0:T(8,128)} async-done(((f32[1024,64]{1,0:T(8,128)}), f32[32,64]{1,0:T(8,128)}) %reduce-scatter.26.cloned.1.call-update) | async-done | bytes 8208 | tf_op jit(solution)/shard_map/reduce_scatter | solution.py:371
  1482.9 137.2 %reduce-scatter.24.cloned.1.call-done = f32[32,96]{1,0:T(8,128)} async-done(((f32[1024,96]{1,0:T(8,128)}), f32[32,96]{1,0:T(8,128)}) %reduce-scatter.24.cloned.1.call-update) | async-done | bytes 12304 | tf_op jit(solution)/shard_map/reduce_scatter | solution.py:370
  1620.2 136.9 %reduce-scatter.22.cloned.1.call-done = f32[32,128]{1,0:T(8,128)} async-done(((f32[1024,128]{1,0:T(8,128)}), f32[32,128]{1,0:T(8,128)}) %reduce-scatter.22.cloned.1.call-update) | async-done | bytes 16400 | tf_op jit(solution)/shard_map/reduce_scatter | solution.py:369
  1757.1 103.8 %reduce-scatter.16.cloned.1.call-done = f32[64,1024]{1,0:T(8,128)} async-done(((f32[1024,1024]{1,0:T(8,128)}), f32[64,1024]{1,0:T(8,128)}) %reduce-scatter.16.cloned.1.call-update) | async-done | bytes 262160 | tf_op jit(solution)/shard_map/reduce_scatter | solution.py:362
  1861.0 211.3 %reduce-scatter.14.cloned.1.call-done = f32[64,3072]{1,0:T(8,128)} async-done(((f32[1024,3072]{1,0:T(8,128)}), f32[64,3072]{1,0:T(8,128)}) %reduce-scatter.14.cloned.1.call-update) | async-done | bytes 786448 | tf_op jit(solution)/shard_map/reduce_scatter | solution.py:361
  2072.2 354.3 %reduce-scatter.18.cloned.1.call-done = f32[64,4096]{1,0:T(8,128)} async-done(((f32[1024,4096]{1,0:T(8,128)}), f32[64,4096]{1,0:T(8,128)}) %reduce-scatter.18.cloned.1.call-update) | async-done | bytes 1048592 | tf_op jit(solution)/shard_map/reduce_scatter | solution.py:363
  2426.6 354.9 %reduce-scatter.20.cloned.1.call-done = f32[256,1024]{1,0:T(8,128)} async-done(((f32[4096,1024]{1,0:T(8,128)}), f32[256,1024]{1,0:T(8,128)}) %reduce-scatter.20.cloned.1.call-update) | async-done | bytes 1048592 | tf_op jit(solution)/shard_map/reduce_scatter | solution.py:364
  (955 shorter events, 314.2 us)
Async XLA Ops:
  7.2 181.3 %all-gather.5.cloned.1.call-start = ((), (), s32[]{:S(2)}) async-start(), calls=%async_computation.11 | async-start | bytes 6684672 | tf_op jit(solution)/shard_map/all_gather | solution.py:273
  9.3 43.5 %copy-start.258 = (s32[2,32]{1,0:T(2,128)S(1)}, s32[2,32]{1,0:T(2,128)}, u32[]{:S(2)}) copy-start(s32[2,32]{1,0:T(2,128)} %param.14) | copy-start | bytes 772
  9.3 196.1 %all-gather.7.cloned.1.call-start = ((), (), s32[]{:S(2)}) async-start(), calls=%async_computation.12 | async-start | bytes 2228224 | tf_op jit(solution)/shard_map/all_gather | solution.py:274
  11.0 282.5 %all-gather.9.cloned.1.call-start = ((), (), s32[]{:S(2)}) async-start(), calls=%async_computation.13 | async-start | bytes 8912896 | tf_op jit(solution)/shard_map/all_gather | solution.py:275
  13.2 128.2 %copy-start.260 = (f32[1,2,64]{2,1,0:T(2,128)S(1)}, f32[1,2,64]{2,1,0:T(2,128)}, u32[]{:S(2)}) copy-start(f32[1,2,64]{2,1,0:T(2,128)} %param.20) | copy-start | bytes 1540
  13.2 128.2 %copy-start.196 = (f32[32,128]{1,0:T(8,128)S(1)}, f32[32,128]{1,0:T(8,128)}, u32[]{:S(2)}) copy-start(f32[32,128]{1,0:T(8,128)} %param.21) | copy-start | bytes 49156
  13.2 128.2 %copy-start.197 = (f32[32,64]{1,0:T(8,128)S(1)}, f32[32,64]{1,0:T(8,128)}, u32[]{:S(2)}) copy-start(f32[32,64]{1,0:T(8,128)} %param.23) | copy-start | bytes 24580
  13.2 394.6 %all-gather.11.cloned.1.call-start = ((), (), s32[]{:S(2)}) async-start(), calls=%async_computation.14 | async-start | bytes 8912896 | tf_op jit(solution)/shard_map/all_gather | solution.py:276
  14.2 174.3 %collective-permute-start = (bf16[2,192,512]{2,1,0:T(8,128)(2,1)S(1)}, bf16[2,192,512]{2,1,0:T(8,128)(2,1)S(1)}, u32[]{:S(2)}, u32[]{:S(2)}) collective-permute-start(bf16[2,192,512]{2,1,0:T(8,128)(2,1)S(1)} %copy-done.136), channel_id=1, source_target_pairs={{16,0},{17,1},{18,2},{19,3},{20,4},{21,5},{22,6},{23,7},{24,8},{25... | collective-permute-start | bytes 1179656 | tf_op jit(solution)/shard_map/ppermute | solution.py:45
  53.5 88.0 %copy-start.165 = (f32[32,64]{0,1:T(8,128)}, f32[32,64]{0,1:T(8,128)S(1)}, u32[]{:S(2)}) copy-start(f32[32,64]{0,1:T(8,128)S(1)} %fusion.269) | copy-start | bytes 24580
  54.2 87.2 %copy-start.178 = (s32[128]{0:T(128)}, s32[128]{0:T(128)S(1)}, u32[]{:S(2)}) copy-start(s32[128]{0:T(128)S(1)} %get-tuple-element.236) | copy-start | bytes 1540
  54.2 87.2 %copy-start.179 = (s32[128]{0:T(128)}, s32[128]{0:T(128)S(1)}, u32[]{:S(2)}) copy-start(s32[128]{0:T(128)S(1)} %get-tuple-element.237) | copy-start | bytes 1540
  57.1 147.3 %copy-start.124 = (pred[192,192]{0,1:T(8,128)(4,1)}, pred[192,192]{0,1:T(8,128)(4,1)S(1)}, u32[]{:S(2)}) copy-start(pred[192,192]{0,1:T(8,128)(4,1)S(1)} %broadcast_compare_fusion.3) | copy-start | bytes 110596
  63.3 504.9 %copy-start.155 = (f32[1024]{0:T(1024)}, f32[1024]{0:T(1024)S(1)}, u32[]{:S(2)}) copy-start(f32[1024]{0:T(1024)S(1)} %get-tuple-element.30) | copy-start | bytes 12292
  63.3 519.2 %copy-start.137 = (f32[1024]{0:T(1024)}, f32[1024]{0:T(1024)S(1)}, u32[]{:S(2)}) copy-start(f32[1024]{0:T(1024)S(1)} %get-tuple-element.29) | copy-start | bytes 12292
  188.5 379.7 %copy-start.167 = (f32[1024]{0:T(1024)}, f32[1024]{0:T(1024)S(1)}, u32[]{:S(2)}) copy-start(f32[1024]{0:T(1024)S(1)} %get-tuple-element.32) | copy-start | bytes 12292
  188.5 394.0 %copy-start.176 = (f32[1024]{0:T(1024)}, f32[1024]{0:T(1024)S(1)}, u32[]{:S(2)}) copy-start(f32[1024]{0:T(1024)S(1)} %get-tuple-element.31) | copy-start | bytes 12292
  188.5 367.1 %copy-start.24 = (bf16[2,192,1024]{2,1,0:T(8,128)(2,1)}, bf16[2,192,1024]{2,1,0:T(8,128)(2,1)S(1)}, u32[]{:S(2)}) copy-start(bf16[2,192,1024]{2,1,0:T(8,128)(2,1)S(1)} %constant_dynamic-update-slice_fusion) | copy-start | bytes 2359300
  207.9 97.9 %copy-start.29 = (f32[192,1024]{1,0:T(8,128)}, f32[192,1024]{1,0:T(8,128)S(1)}, u32[]{:S(2)}) copy-start(f32[192,1024]{1,0:T(8,128)S(1)} %get-tuple-element.176) | copy-start | bytes 2359300
  208.4 199.4 %copy-start.31 = (f32[192,1024]{1,0:T(8,128)}, f32[192,1024]{1,0:T(8,128)S(1)}, u32[]{:S(2)}) copy-start(f32[192,1024]{1,0:T(8,128)S(1)} %multiply_add_fusion.6) | copy-start | bytes 2359300
  407.8 148.0 %slice-start = ((s8[6291456]{0:T(1024)(128)(4,1)}), s8[4194304]{0:T(1024)(128)(4,1)S(1)}, s32[]{:S(2)}) async-start(s8[6291456]{0:T(1024)(128)(4,1)} %bitcast.379), calls=%async_computation.24 | async-start | bytes 8388608
  407.8 148.0 %slice-start.1 = ((s8[6291456]{0:T(1024)(128)(4,1)}), s8[2097152]{0:T(1024)(128)(4,1)S(1)}, s32[]{:S(2)}) async-start(s8[6291456]{0:T(1024)(128)(4,1)} %bitcast.379), calls=%async_computation.25 | async-start | bytes 4194304
  414.9 140.7 %collective-permute-start.1 = (bf16[192,1024]{1,0:T(8,128)(2,1)S(1)}, bf16[192,1024]{1,0:T(8,128)(2,1)S(1)}, u32[]{:S(2)}, u32[]{:S(2)}) collective-permute-start(bf16[192,1024]{1,0:T(8,128)(2,1)S(1)} %add_convert_fusion.8), channel_id=1, source_target_pairs={{0,16},{1,17},{2,18},{3,19},{4,20},{5,21},{6,22},{7,23},{8,24},{9,... | collective-permute-start | bytes 1179656 | tf_op jit(solution)/shard_map/ppermute | solution.py:45
  555.8 277.8 %copy-start.1 = (bf16[192,1024]{1,0:T(8,128)(2,1)}, bf16[192,1024]{1,0:T(8,128)(2,1)S(1)}, u32[]{:S(2)}) copy-start(bf16[192,1024]{1,0:T(8,128)(2,1)S(1)} %broadcast_select_fusion.16) | copy-start | bytes 1179652
  582.7 139.7 %copy-start.7 = (bf16[192,1024]{1,0:T(8,128)(2,1)}, bf16[192,1024]{1,0:T(8,128)(2,1)S(1)}, u32[]{:S(2)}) copy-start(bf16[192,1024]{1,0:T(8,128)(2,1)S(1)} %add_convert_fusion.7) | copy-start | bytes 1179652
  582.7 228.6 %collective-permute-start.2 = (bf16[192,1024]{1,0:T(8,128)(2,1)S(1)}, bf16[192,1024]{1,0:T(8,128)(2,1)}, u32[]{:S(2)}, u32[]{:S(2)}) collective-permute-start(bf16[192,1024]{1,0:T(8,128)(2,1)S(1)} %add_convert_fusion.7), channel_id=1, source_target_pairs={{0,16},{1,17},{2,18},{3,19},{4,20},{5,21},{6,22},{7,23},{8,24},{9,... | collective-permute-start | bytes 1179656 | tf_op jit(solution)/shard_map/ppermute | solution.py:45
  797.0 57.7 %all-to-all-start = ((bf16[16,64,288]{2,1,0:T(8,128)(2,1)}), bf16[16,64,288]{2,1,0:T(8,128)(2,1)}, u32[]{:S(2)}, u32[]{:S(2)}) async-start(bf16[16,64,288]{2,1,0:T(8,128)(2,1)} %bitcast.418), calls=%async_computation | async-start | bytes 1572864 | tf_op jit(solution)/shard_map/all_to_all | solution.py:31
  812.3 24.8 copy-start.3
  835.4 14.6 copy-start.57
  835.4 14.6 copy-start.203
  849.9 20.5 copy-start.43
  1071.0 19.3 copy-start.245
  1080.1 51.7 %all-to-all-start.1 = ((bf16[16,64,288]{2,1,0:T(8,128)(2,1)}), bf16[16,64,288]{2,1,0:T(8,128)(2,1)}, u32[]{:S(2)}, u32[]{:S(2)}) async-start(bf16[16,64,288]{2,1,0:T(8,128)(2,1)} %bitcast.419), calls=%async_computation.1 | async-start | bytes 1572864 | tf_op jit(solution)/shard_map/all_to_all | solution.py:31
  1090.2 266.4 %reduce-scatter.28.cloned.1.call-start = ((), (), s32[]{:S(2)}) async-start(), calls=%async_computation.22 | async-start | bytes 557056
  1127.8 15.9 collective-permute-start.4
  1143.7 17.1 slice-start.16
  1179.5 4.3 collective-permute-start.5
  1180.8 16.4 slice-start.18
  1203.1 155.0 %reduce-scatter.30.cloned.1.call-start = ((), (), s32[]{:S(2)}) async-start(), calls=%async_computation.23 | async-start | bytes 557056
  1204.9 278.0 %reduce-scatter.26.cloned.1.call-start = ((), (), s32[]{:S(2)}) async-start(), calls=%async_computation.21 | async-start | bytes 540672 | tf_op jit(solution)/shard_map/reduce_scatter | solution.py:371
  1207.2 413.0 %reduce-scatter.24.cloned.1.call-start = ((), (), s32[]{:S(2)}) async-start(), calls=%async_computation.20 | async-start | bytes 540672 | tf_op jit(solution)/shard_map/reduce_scatter | solution.py:370
  1213.7 543.5 %reduce-scatter.22.cloned.1.call-start = ((), (), s32[]{:S(2)}) async-start(), calls=%async_computation.19 | async-start | bytes 540672 | tf_op jit(solution)/shard_map/reduce_scatter | solution.py:369
  1219.4 641.6 %reduce-scatter.16.cloned.1.call-start = ((), (), s32[]{:S(2)}) async-start(), calls=%async_computation.16 | async-start | bytes 4456448 | tf_op jit(solution)/shard_map/reduce_scatter | solution.py:362
  1228.4 843.8 %reduce-scatter.14.cloned.1.call-start = ((), (), s32[]{:S(2)}) async-start(), calls=%async_computation.15 | async-start | bytes 13369344 | tf_op jit(solution)/shard_map/reduce_scatter | solution.py:361
  1267.7 1158.9 %reduce-scatter.18.cloned.1.call-start = ((), (), s32[]{:S(2)}) async-start(), calls=%async_computation.17 | async-start | bytes 17825792 | tf_op jit(solution)/shard_map/reduce_scatter | solution.py:363
  1305.9 1475.6 %reduce-scatter.20.cloned.1.call-start = ((), (), s32[]{:S(2)}) async-start(), calls=%async_computation.18 | async-start | bytes 17825792 | tf_op jit(solution)/shard_map/reduce_scatter | solution.py:364
  1351.3 8.2 collective-permute-start.6
  1353.0 3.0 collective-permute-start.3
  (257 other events, 1216.0 us)
Sparse Core Ops, SparseCore 0:
  11.4 99.9 all-gather.4
  114.7 63.6 all-gather.6
  181.8 111.7 all-gather.8
  296.7 111.0 all-gather.10
  1203.2 66.6 reduce-scatter.27
  1272.0 72.8 reduce-scatter.29
  1347.8 135.1 reduce-scatter.25
  1485.8 134.2 reduce-scatter.23
  1623.0 134.0 reduce-scatter.21
  1759.9 100.9 reduce-scatter.15
  1868.1 204.0 reduce-scatter.13
  2075.0 351.5 reduce-scatter.17
  2429.4 352.0 reduce-scatter.19
where the time goes:
time: 2800 us; the launch traced here: 2790 us
  waiting for transfers between devices  1610 us (58%)
  blocking collectives  603 us (22%)
  matrix products  325 us (12%)
  local copies, waits for them, and re-layouts  116 us (4%)
  other arithmetic  82.6 us (3%)
  starting transfers between devices  31.9 us (1%)
    reduce_scatter x1, waiting for transfers between devices, on_device(): lax.psum_scatter(grad_totals[3], 'dp', scatter_dimension=0, tiled=True)  355 us
    reduce_scatter x1, waiting for transfers between devices, on_device(): lax.psum_scatter(grad_totals[2], 'dp', scatter_dimension=0, tiled=True)  354 us
    reduce_scatter x1, waiting for transfers between devices, on_device(): lax.psum_scatter(grad_totals[0], 'dp', scatter_dimension=0, tiled=True)  211 us
    reduce_scatter x1, waiting for transfers between devices, on_device(): lax.psum_scatter(head_sums[1], ('section', 'dp'), scatter_dimension=0, ti...  137 us
    reduce_scatter x1, waiting for transfers between devices, on_device(): lax.psum_scatter(head_sums[0], ('section', 'dp'), scatter_dimension=0, ti...  137 us
    dot_general x24, matrix products, dot_left_t(): lax.dot_general(left, right, (((0,), (0,)), ((), ())), preferred_element_...  133 us
    reduce_scatter x1, waiting for transfers between devices, on_device(): lax.psum_scatter(head_sums[2], ('section', 'dp'), scatter_dimension=0, ti...  122 us
    reduce_scatter x1, waiting for transfers between devices, on_device(): lax.psum_scatter(grad_totals[1], 'dp', scatter_dimension=0, tiled=True)  104 us
  transfers between devices with their start and end apart: 22, of which 11 were waited for; matrix products, arithmetic and copies ran while one was open for 12% of the time, Pallas kernels for 0%

commit v1 on v0

v1 whole, which is shorter than its diff:
```python
import math

import jax
import jax.numpy as jnp
from jax import lax
from jax.sharding import PartitionSpec as P

D = 1024
DH = 64
ROW = 128
NSEG = 4
QDEV = 2
QLEN = 32
WIDTHS = (128, 96, 64)

ln_eps = 1e-05
norm_eps = 1e-06
sharpness = 16.0
masked_score = -1000000000.0
highest = lax.Precision.HIGHEST
bf16 = jnp.bfloat16
f32 = jnp.float32


def factors(count, ways):
    sizes = [1] * ways
    left = count
    while left > 1:
        at = min(range(ways), key=lambda i: (sizes[i], i))
        sizes[at] *= 2
        left //= 2
    return tuple(sorted(sizes, reverse=True))


def route(dims, axis, step):
    stride = math.prod(dims[axis + 1 :])
    pairs = []
    for source in range(math.prod(dims)):
        digit = source // stride % dims[axis]
        pairs.append((source, source + ((digit ^ step) - digit) * stride))
    return pairs


def digits_of(dims):
    index = lax.axis_index("dp")
    return [index // math.prod(dims[a + 1 :]) % dims[a] for a in range(len(dims))]


def gather_blocks(shard, dims, order):
    digits = digits_of(dims)
    have = shard.reshape((1,) * len(dims) + shard.shape)
    for axis in order:
        count = dims[axis]
        if count == 1:
            continue
        parts = [have] + [
            lax.ppermute(have, "dp", route(dims, axis, k)) for k in range(1, count)
        ]
        if count == 2:
            have = jnp.where(
                digits[axis] == 0,
                jnp.concatenate(parts, axis),
                jnp.concatenate(parts[::-1], axis),
            )
        else:
            stacked = jnp.concatenate(parts, axis)
            have = jnp.concatenate(
                [
                    lax.dynamic_slice_in_dim(stacked, digits[axis] ^ j, 1, axis)
                    for j in range(count)
                ],
                axis,
            )
    return have


def scatter_blocks(total, dims, order, wire):
    digits = digits_of(dims)
    for axis in order:
        count = dims[axis]
        if count == 1:
            continue
        own = lax.dynamic_slice_in_dim(total, digits[axis], 1, axis)
        for k in range(1, count):
            part = lax.dynamic_slice_in_dim(total, digits[axis] ^ k, 1, axis).astype(wire)
            own = own + lax.ppermute(part, "dp", route(dims, axis, k)).astype(f32)
        total = own
    return total.reshape(total.shape[len(dims) :])


def swap(value):
    return lax.ppermute(value, "section", [(0, 1), (1, 0)])


def one_way(value, source):
    return lax.ppermute(value, "section", [(source, 1 - source)])


def by_core(is_first, mine, other, axis):
    return jnp.where(
        is_first,
        jnp.concatenate([mine, other], axis),
        jnp.concatenate([other, mine], axis),
    )


def layout(row_lengths):
    ends = jnp.cumsum(row_lengths)
    starts = ends - row_lengths
    places = jnp.arange(ROW, dtype=jnp.int32)
    doc_seg = jnp.sum((places[:, None] >= ends[None, :]).astype(jnp.int32), axis=1)
    owners = doc_seg[:, None] == jnp.arange(NSEG + 1, dtype=jnp.int32)[None, :]
    doc_pos = places - jnp.sum(jnp.where(owners, starts[None, :], 0), axis=1)
    query_places = jnp.arange(QDEV * QLEN, dtype=jnp.int32)
    query_seg = NSEG + 1 + query_places // QLEN
    query_pos = query_places % QLEN
    segment_ids = jnp.concatenate([doc_seg, query_seg])
    positions = jnp.concatenate([doc_pos, query_pos])
    return (segment_ids, positions)


def rotary(positions):
    half_dim = DH // 2
    freqs = jnp.exp(jnp.arange(half_dim, dtype=f32) * (-math.log(10000.0) / half_dim))
    angles = positions.astype(f32)[..., None] * freqs
    cosine = jnp.cos(angles)
    sine = jnp.sin(angles)
    return (jnp.concatenate([cosine, cosine], -1), jnp.concatenate([sine, sine], -1))


def rope(values, cosine, sine):
    half_dim = values.shape[-1] // 2
    turned = jnp.concatenate([-values[..., half_dim:], values[..., :half_dim]], -1)
    return values * cosine[..., None, :] + turned * sine[..., None, :]


def rope_back(grads, cosine, sine):
    half_dim = grads.shape[-1] // 2
    scaled = grads * sine[..., None, :]
    turned = jnp.concatenate([scaled[..., half_dim:], -scaled[..., :half_dim]], -1)
    return grads * cosine[..., None, :] + turned


def normalize(values):
    centre = values - jnp.mean(values, -1, keepdims=True)
    scale = lax.rsqrt(jnp.mean(centre * centre, -1, keepdims=True) + ln_eps)
    return centre * scale, scale


def normalize_back(grad, gain, normal, scale):
    inner = grad * gain
    mean_inner = jnp.mean(inner, -1, keepdims=True)
    mean_mixed = jnp.mean(inner * normal, -1, keepdims=True)
    return (
        scale * (inner - mean_inner - normal * mean_mixed),
        jnp.sum(grad * normal, 0),
        jnp.sum(grad, 0),
    )


def gelu(values):
    return 0.5 * values * (1.0 + lax.erf(values * math.sqrt(0.5)))


def gelu_slope(values):
    density = jnp.exp(-0.5 * values * values) * (1.0 / math.sqrt(2.0 * math.pi))
    return 0.5 * (1.0 + lax.erf(values * math.sqrt(0.5))) + values * density


def dot_plain(left, right):
    return jnp.dot(left, right, preferred_element_type=f32)


def dot_left_t(left, right):
    return lax.dot_general(left, right, (((0,), (0,)), ((), ())), preferred_element_type=f32)


def dot_right_t(left, right):
    return lax.dot_general(left, right, (((1,), (1,)), ((), ())), preferred_element_type=f32)


def masked_scores(q_rot, k_rot, same):
    scores = jnp.einsum("mthd,muhd->mhtu", q_rot, k_rot, preferred_element_type=f32) * 0.125
    return jnp.where(same[:, None], scores, masked_score)


def softmax_rows(scores):
    raised = jnp.exp(scores - jnp.max(scores, -1, keepdims=True))
    return raised / jnp.sum(raised, -1, keepdims=True)


def layer_ahead(entry, weights, norms, where):
    w_qkv, w_out, w_up, w_down = weights
    gains, biases = norms
    is_first, same, cosine, sine = where
    rows = entry.shape[0] // 2
    mixed = dot_plain(entry, w_qkv)
    width = mixed.shape[1] // 3

    def heads_of(values):
        return values.reshape(2, rows, width // DH, DH)

    q_rot = rope(heads_of(mixed[:, :width]), cosine, sine).astype(bf16)
    k_rot = rope(heads_of(mixed[:, width : 2 * width]), cosine, sine).astype(bf16)
    v_low = heads_of(mixed[:, 2 * width :]).astype(bf16)
    soft = softmax_rows(masked_scores(q_rot, k_rot, same))
    attended = jnp.einsum("mhtu,muhd->mthd", soft.astype(bf16), v_low, preferred_element_type=f32)
    o_half = attended.reshape(2 * rows, width).astype(bf16)
    o_other = swap(jnp.concatenate([o_half[rows:], o_half[:rows]], 0))
    o_full = by_core(is_first, o_half, o_other, 1)
    branch = dot_plain(o_full[:rows], w_out)
    normal_one, scale_one = normalize(entry[:rows].astype(f32) + branch)
    middle = normal_one * gains[0] + biases[0]
    middle_low = middle.astype(bf16)
    middle_both = jnp.concatenate([middle_low, swap(middle_low)], 0)
    raised = dot_plain(middle_both, w_up)
    active = gelu(raised).astype(bf16)
    lowered = dot_plain(active, w_down)
    lowered = lowered[:rows] + swap(lowered[rows:])
    normal_two, scale_two = normalize(middle + lowered)
    result = normal_two * gains[1] + biases[1]
    kept = (entry, q_rot, k_rot, v_low, o_full, normal_one, scale_one, middle_both, raised, active)
    return result, kept + (normal_two, scale_two)


def layer_back(grad, kept, weights, norms, where, block_rows):
    entry, q_rot, k_rot, v_low, o_full, normal_one, scale_one, middle_both, raised, active = kept[:10]
    normal_two, scale_two = kept[10:]
    w_qkv, w_out, w_up, w_down = weights
    gains, _ = norms
    is_first, same, cosine, sine = where
    rows = grad.shape[0]
    d_two, d_gain_two, d_bias_two = normalize_back(grad, gains[1], normal_two, scale_two)
    d_low = d_two.astype(bf16)
    d_lowered = jnp.concatenate([d_low, swap(d_low)], 0)
    g_down = dot_left_t(active, d_lowered)
    d_active = dot_right_t(d_lowered, w_down)
    d_raised = (d_active * gelu_slope(raised)).astype(bf16)
    g_up = dot_left_t(middle_both, d_raised)
    d_middle = dot_right_t(d_raised, w_up)
    d_middle = d_two + d_middle[:rows] + swap(d_middle[rows:])
    d_one, d_gain_one, d_bias_one = normalize_back(d_middle, gains[0], normal_one, scale_one)
    d_low = d_one.astype(bf16)
    d_branch = jnp.concatenate([d_low, swap(d_low)], 0)
    half = D // 2
    g_out = dot_left_t(o_full, jnp.where(is_first, d_branch[:, :half], d_branch[:, half:]))
    w_mine = jnp.where(is_first, w_out[:half], w_out[half:])
    d_attended = dot_right_t(d_branch, w_mine).astype(bf16)
    d_attended = d_attended.reshape(v_low.shape)
    soft = softmax_rows(masked_scores(q_rot, k_rot, same))
    d_soft = jnp.einsum("mthd,muhd->mhtu", d_attended, v_low, preferred_element_type=f32)
    d_value = jnp.einsum(
        "mhtu,mthd->muhd", soft.astype(bf16), d_attended, preferred_element_type=f32
    )
    inner = jnp.sum(soft * d_soft, -1, keepdims=True)
    d_scores = (soft * (d_soft - inner)).astype(bf16)
    d_query = jnp.einsum("mhtu,muhd->mthd", d_scores, k_rot, preferred_element_type=f32) * 0.125
    d_key = jnp.einsum("mhtu,mthd->muhd", d_scores, q_rot, preferred_element_type=f32) * 0.125
    d_mixed = jnp.concatenate(
        [
            part.reshape(2 * rows, -1).astype(bf16)
            for part in (
                rope_back(d_query, cosine, sine),
                rope_back(d_key, cosine, sine),
                d_value,
            )
        ],
        axis=1,
    )
    g_qkv = dot_left_t(entry, d_mixed)
    d_entry = dot_right_t(d_mixed, w_qkv)
    norm_grads = (d_gain_one, d_gain_two, d_bias_one, d_bias_two)
    return d_one, d_entry, (g_qkv, g_out, g_up, g_down), norm_grads


def head_pass(final, heads, segments, labels_row, small):
    dp_index = lax.axis_index("dp")
    flat_rows = final.astype(bf16)
    cuts = [sum(WIDTHS[:k]) for k in range(4)]
    spans = [(cuts[k], cuts[k + 1]) for k in range(3)]
    member = (segments[:ROW, None] == jnp.arange(NSEG, dtype=jnp.int32)[None, :]).astype(f32)
    embedded = dot_plain(flat_rows, heads)
    inverse = [
        lax.rsqrt(jnp.sum(jnp.square(embedded[:, a:b]), -1, keepdims=True) + norm_eps)
        for a, b in spans
    ]
    exact = [embedded[:, a:b] * inverse[k] for k, (a, b) in enumerate(spans)]
    units = jnp.concatenate(exact, 1).astype(bf16)
    everyone = gather_blocks(units[ROW:], small, range(len(small)))
    everyone = everyone.reshape(-1, units.shape[1])
    exponents = []
    masses = []
    local = []
    for a, b in spans:
        similar = dot_right_t(units[:ROW, a:b], everyone[:, a:b])
        expo = jnp.exp(sharpness * similar)
        mass = lax.dot_general(member, expo, (((0,), (0,)), ((), ())), precision=highest)
        exponents.append(expo)
        masses.append(mass)
        local.append(jnp.sum((jnp.log(mass) / sharpness).reshape(NSEG, -1, QLEN), -1))
    local = jnp.stack(local)
    logits = gather_blocks(local, small, range(len(small)))
    logits = jnp.moveaxis(logits.reshape((-1,) + local.shape), 0, 1)
    logits = logits.reshape(3, -1, local.shape[2])
    label_hot = jnp.arange(logits.shape[1], dtype=jnp.int32)[:, None] == labels_row[None, :]
    label_hot = label_hot.astype(f32)
    peak = jnp.max(logits, 1, keepdims=True)
    spread = jnp.exp(logits - peak)
    totals = jnp.sum(spread, 1, keepdims=True)
    per_query = jnp.sum(peak[:, 0] + jnp.log(totals[:, 0]) - jnp.sum(logits * label_hot, 1), 0)
    own_losses = lax.dynamic_slice_in_dim(per_query, dp_index * QDEV, QDEV)
    d_logits = spread / totals - label_hot
    d_local = lax.dynamic_slice_in_dim(d_logits, dp_index * NSEG, NSEG, 1)
    d_queries = []
    d_docs = []
    for k, (a, b) in enumerate(spans):
        d_mass = jnp.repeat(d_local[k], QLEN, axis=1) / (sharpness * masses[k])
        d_expo = jnp.dot(member, d_mass, precision=highest)
        d_similar = (d_expo * exponents[k] * sharpness).astype(bf16)
        d_queries.append(dot_left_t(d_similar, units[:ROW, a:b]))
        d_docs.append(dot_plain(d_similar, everyone[:, a:b]))
    d_queries = jnp.concatenate(d_queries, 1)
    d_queries = d_queries.reshape(small + (-1,) + d_queries.shape[1:])
    back = scatter_blocks(d_queries, small, range(len(small))[::-1], bf16)
    d_unit = jnp.concatenate([jnp.concatenate(d_docs, 1), back], 0)
    d_embedded = []
    for k, (a, b) in enumerate(spans):
        along = jnp.sum(d_unit[:, a:b] * exact[k], -1, keepdims=True)
        d_embedded.append((d_unit[:, a:b] - exact[k] * along) * inverse[k])
    d_embedded = jnp.concatenate(d_embedded, 1).astype(bf16)
    return own_losses, dot_right_t(d_embedded, heads), dot_left_t(flat_rows, d_embedded)


def halves_of(mine, is_first):
    kept = jnp.where(is_first, mine[0], mine[1])
    other = swap(jnp.where(is_first, mine[1], mine[0]))
    return jnp.where(is_first, kept, other), jnp.where(is_first, other, kept)


def on_device(
    inputs, lengths, labels, w_qkv, w_out, w_up, w_down, ln_gain, ln_bias, head_a, head_b, head_c
):
    peers = lax.axis_size("dp")
    dims = factors(peers, 3)
    small = factors(peers, 2)
    is_first = lax.axis_index("section") == 0
    rows = inputs.shape[1]
    block = w_qkv.shape[1]
    unit_block = w_down.shape[1] // 2

    qkv_half = w_qkv[0].astype(bf16).reshape(block, 3, 2, D // 2)
    qkv_half = jnp.moveaxis(qkv_half, 2, 0).reshape(2, block, -1)
    out_half = jnp.moveaxis(w_out[0].astype(bf16).reshape(block, 2, D // 2), 1, 0)
    up_half = w_up[0].astype(bf16).reshape(block, peers, 2, unit_block)
    up_half = jnp.moveaxis(up_half, 2, 0).reshape(2, block, -1)
    down_half = w_down[0].astype(bf16).reshape(2, unit_block, D)
    attn_parts = halves_of(jnp.concatenate([qkv_half, out_half], 2), is_first)
    up_parts = halves_of(up_half, is_first)
    down_parts = halves_of(down_half, is_first)

    norm_mine = jnp.concatenate([ln_gain[0], ln_bias[0]], 0).astype(bf16)
    norm_both = by_core(is_first, norm_mine[None], swap(norm_mine)[None], 0)
    norms = gather_blocks(norm_both, small, range(len(small)))
    norms = jnp.moveaxis(norms.reshape((peers,) + norm_both.shape), 0, 2)
    norms = norms.reshape(2, 4, D).astype(f32)
    head_mine = jnp.concatenate([head_a, head_b, head_c], 1).astype(bf16)
    head_both = by_core(is_first, head_mine[None], swap(head_mine)[None], 0)
    heads = gather_blocks(head_both, small, range(len(small)))
    heads = jnp.moveaxis(heads.reshape((peers,) + head_both.shape), 0, 1).reshape(D, -1)

    orders = ((0, 1, 2), (0, 2, 1))
    weights = []
    for l in range(2):
        attn = gather_blocks(attn_parts[l], dims, orders[l]).reshape(D, -1)
        up = gather_blocks(up_parts[l], dims, orders[1 - l]).reshape(D, -1)
        down = gather_blocks(down_parts[l], dims, orders[l]).reshape(-1, D)
        out_mine = attn[:, 3 * D // 2 :]
        out = by_core(is_first, out_mine, swap(out_mine), 1)
        weights.append((attn[:, : 3 * D // 2], out, up, down))

    whole = by_core(is_first, inputs, swap(inputs), 2)
    entry = jnp.where(is_first, whole, whole[::-1]).reshape(2 * rows, D)
    own_lengths = jnp.where(is_first, lengths, lengths[::-1])[:, 0]
    segments, positions = jax.vmap(layout)(own_lengths)
    cosine, sine = rotary(positions)
    same = segments[:, :, None] == segments[:, None, :]
    where = (is_first, same, cosine, sine)
    labels_own = jnp.where(is_first, labels[0], labels[1])

    kept = []
    pairs = [((norms[l, 0], norms[l, 1]), (norms[l, 2], norms[l, 3])) for l in range(2)]
    for l in range(2):
        result, saved = layer_ahead(entry, weights[l], pairs[l], where)
        kept.append(saved)
        if l == 0:
            low = result.astype(bf16)
            entry = jnp.concatenate([low, swap(low)], 0)
    losses, grad, g_heads = head_pass(result, heads, segments[0], labels_own, small)

    shards = [None, None]
    norm_grads = [None, None]
    back = ((2, 1, 0), (1, 2, 0))
    for l in (1, 0):
        d_one, d_entry, grads, norm_grads[l] = layer_back(
            grad, kept[l], weights[l], pairs[l], where, block
        )
        g_qkv, g_out, g_up, g_down = grads
        down = scatter_blocks(g_down.reshape(dims + (unit_block, D)), dims, back[l], bf16)
        up = scatter_blocks(g_up.reshape(dims + (block, -1)), dims, back[1 - l], bf16)
        g_attn = jnp.concatenate([g_qkv, g_out], 1)
        if l == 1:
            g_heads = g_heads.reshape(2, D // 2, -1)
            g_mine = jnp.where(is_first, g_heads[0], g_heads[1])
            g_mine = g_mine + swap(jnp.where(is_first, g_heads[1], g_heads[0]))
            g_mine = g_mine.reshape(D, -1)
            g_attn = jnp.concatenate([g_attn, g_mine], 1)
        attn = scatter_blocks(g_attn.reshape(dims + (block, -1)), dims, back[l], bf16)
        if l == 1:
            head_shard = attn[:, 2 * D :].reshape(D // 2 // peers, -1)
        shards[l] = (attn[:, : 3 * D // 2], attn[:, 3 * D // 2 : 2 * D], up, down)
        if l == 1:
            d_entry = d_one + d_entry[:rows] + swap(d_entry[rows:])
            grad = d_entry.astype(bf16).astype(f32)

    partial = jnp.concatenate([d_entry[:rows] + d_one, d_entry[rows:]], 0).reshape(2, rows, D)
    mine = jnp.where(is_first, partial[..., : D // 2], partial[..., D // 2 :])
    other = swap(jnp.where(is_first, partial[..., D // 2 :], partial[..., : D // 2]))
    grad_inputs = mine + other[::-1]
    grad_inputs = jnp.where(is_first, grad_inputs, grad_inputs[::-1])

    owned = []
    for i in range(4):
        from_first = one_way(shards[1][i], 0)
        from_second = one_way(shards[0][i], 1)
        lower = jnp.where(is_first, shards[0][i], from_first)
        upper = jnp.where(is_first, from_second, shards[1][i])
        owned.append((lower, upper))
    grad_qkv = jnp.stack([h.reshape(block, 3, D // 2) for h in owned[0]], 2).reshape(block, 3 * D)
    grad_out = jnp.concatenate(owned[1], 1)
    grad_up = jnp.stack([h.reshape(block, peers, unit_block) for h in owned[2]], 2)
    grad_up = grad_up.reshape(block, -1)
    grad_down = jnp.concatenate(owned[3], 0)

    norm_all = jnp.stack([jnp.stack(norm_grads[l]) for l in range(2)])
    norm_mine = jnp.where(is_first, norm_all[0], norm_all[1])
    norm_mine = norm_mine + swap(jnp.where(is_first, norm_all[1], norm_all[0]))
    norm_mine = jnp.moveaxis(norm_mine.reshape((4,) + small + (-1,)), 0, len(small))
    norm_shard = scatter_blocks(norm_mine, small, range(len(small))[::-1], f32)

    cross = swap(jnp.where(is_first, losses[1], losses[0])[None])[0]
    kept_loss = jnp.where(is_first, losses[0], losses[1])
    loss_out = jnp.where(
        is_first, jnp.stack([kept_loss, cross]), jnp.stack([cross, kept_loss])
    ).reshape(2, 1, 1)
    head_grads = jnp.split(head_shard, [WIDTHS[0], WIDTHS[0] + WIDTHS[1]], axis=1)
    return (
        loss_out,
        grad_inputs,
        grad_qkv[None],
        grad_out[None],
        grad_up[None],
        grad_down[None],
        norm_shard[None, :2],
        norm_shard[None, 2:],
        head_grads[0],
        head_grads[1],
        head_grads[2],
    )


def solution(mesh):
    placed = (
        P(None, "dp", "section"),
        P(None, "dp", None),
        P(),
        P("section", "dp", None),
        P("section", "dp", None),
        P("section", "dp", None),
        P("section", "dp", None),
        P("section", None, "dp"),
        P("section", None, "dp"),
        P(("section", "dp"), None),
        P(("section", "dp"), None),
        P(("section", "dp"), None),
    )
    return jax.shard_map(
        on_device,
        mesh=mesh,
        in_specs=placed,
        out_specs=(
            P(None, "dp", "section"),
            P(None, "dp", "section"),
            P("section", "dp", None),
            P("section", "dp", None),
            P("section", "dp", None),
            P("section", "dp", None),
            P("section", None, "dp"),
            P("section", None, "dp"),
            P(("section", "dp"), None),
            P(("section", "dp"), None),
            P(("section", "dp"), None),
        ),
        check_vma=False,
    )
```

time: 2800 us -> 981 us (0.35)
  waiting for transfers between devices: 1610 us -> 444 us
  blocking collectives: 603 us -> 0 us
  matrix products: 325 us -> 92.9 us
  starting transfers between devices: 31.9 us -> 145 us
  other arithmetic: 82.6 us -> 149 us
    reduce_scatter x7 -> x0, waiting for transfers between devices: 1420 us -> none  [the longest x1 355 us: on_device(): lax.psum_scatter(grad_totals[3], 'dp', scatter_dimension=0, tiled=True)]
    all_gather x13 -> x0, blocking collectives: 603 us -> none  [the longest x2 86 us: head_pass(): lax.all_gather(unit_list[0][ROW:], 'dp', axis=0, tiled=True)]
    ppermute x7 -> x130, waiting for transfers between devices: 3.61 us -> 444 us  [the longest x54 253 us: gather_blocks(): lax.ppermute(have, 'dp', route(dims, axis, k))]
    all_gather x4 -> x0, waiting for transfers between devices: 187 us -> none  [the longest x1 102 us: on_device(): lax.all_gather(w_down.astype(jnp.bfloat16), 'dp', axis=1, tiled=True)]
    ppermute x7 -> x130, starting transfers between devices: 9.99 us -> 145 us  [the longest x54 72.5 us: gather_blocks(): lax.ppermute(have, 'dp', route(dims, axis, k))]
    dot_general x24 -> x12, matrix products: 133 us -> 21.2 us  [dot_left_t(): lax.dot_general(left, right, (((0,), (0,)), ((), ())), preferred_element_...]
    dot_general x57 -> x30, matrix products: 110 us -> 46.4 us  [the longest x12 22.2 us: dot_plain(): return jnp.dot(left, right, preferred_element_type=f32)]
    dot_general x24 -> x12, matrix products: 82 us -> 25.4 us  [dot_right_t(): lax.dot_general(left, right, (((1,), (1,)), ((), ())), preferred_element_...]
  transfers between devices with their start and end apart: 22 -> 130, of which waited for: 11 -> 60; matrix products, arithmetic and copies ran while one was open for 12% -> 31% of each run, Pallas kernels for 0% -> 0%
where the time goes in v1:
time: 981 us; the launch traced here: 968 us
  waiting for transfers between devices  444 us (45%)
  other arithmetic  149 us (15%)
  starting transfers between devices  145 us (15%)
  local copies, waits for them, and re-layouts  130 us (13%)
  matrix products  92.9 us (9%)
    ppermute x54, waiting for transfers between devices, gather_blocks(): lax.ppermute(have, 'dp', route(dims, axis, k))  253 us
    ppermute x42, waiting for transfers between devices, scatter_blocks(): own = own + lax.ppermute(part, 'dp', route(dims, axis, k)).astype(f32)  188 us
    ppermute x54, starting transfers between devices, gather_blocks(): lax.ppermute(have, 'dp', route(dims, axis, k))  72.5 us
    ppermute x42, starting transfers between devices, scatter_blocks(): own = own + lax.ppermute(part, 'dp', route(dims, axis, k)).astype(f32)  55.1 us
    select_n x12, other arithmetic, gather_blocks(): jnp.where(digits[axis] == 0, jnp.concatenate(parts, axis), jnp.concatenat...  30.8 us
    add x15, other arithmetic, scatter_blocks(): own = own + lax.ppermute(part, 'dp', route(dims, axis, k)).astype(f32)  29.9 us
    unnamed x367, local copies, waits for them, and re-layouts  28.7 us
    dot_general x12, matrix products, dot_right_t(): lax.dot_general(left, right, (((1,), (1,)), ((), ())), preferred_element_...  25.4 us
  transfers between devices with their start and end apart: 130, of which 60 were waited for; matrix products, arithmetic and copies ran while one was open for 31% of the time, Pallas kernels for 0%

profile of v1, /device:TPU:10, one launch (start us, length us, event | category | flops | bytes accessed | tf_op | source)
XLA Modules:
  0.0 967.7 jit_solution(14513331531306514293)
XLA Ops:
  46.2 12.4 %collective-permute-done.4 = bf16[1,1,1,64,2048]{4,3,2,1,0:T(8,128)(2,1)S(1)} collective-permute-done((bf16[1,1,1,64,2048]{4,3,2,1,0:T(8,128)(2,1)S(1)}, bf16[1,1,1,64,2048]{4,3,2,1,0:T(8,128)(2,1)S(1)}, u32[]{:S(2)}, u32[]{:S(2)}) %collective-permute-start.4) | collective-permute-done | bytes 262176 | tf_op jit(solution)/shard_map/ppermute | solution.py:57
  58.8 14.7 %collective-permute-done.3 = bf16[1,1,1,64,2048]{4,3,2,1,0:T(8,128)(2,1)S(1)} collective-permute-done((bf16[1,1,1,64,2048]{4,3,2,1,0:T(8,128)(2,1)S(1)}, bf16[1,1,1,64,2048]{4,3,2,1,0:T(8,128)(2,1)S(1)}, u32[]{:S(2)}, u32[]{:S(2)}) %collective-permute-start.3) | collective-permute-done | bytes 262176 | tf_op jit(solution)/shard_map/ppermute | solution.py:57
  75.1 4.3 collective-permute-start.32
  79.5 18.5 %collective-permute-done.20 = bf16[1,1,1,64,2048]{4,3,2,1,0:T(8,128)(2,1)S(1)} collective-permute-done((bf16[1,1,1,64,2048]{4,3,2,1,0:T(8,128)(2,1)S(1)}, bf16[1,1,1,64,2048]{4,3,2,1,0:T(8,128)(2,1)S(1)}, u32[]{:S(2)}, u32[]{:S(2)}) %collective-permute-start.20) | collective-permute-done | bytes 262176 | tf_op jit(solution)/shard_map/ppermute | solution.py:57
  101.7 3.4 collective-permute-start.45
  105.6 26.1 %collective-permute-done.46 = bf16[1,1,1,128,1024]{4,3,2,1,0:T(8,128)(2,1)S(1)} collective-permute-done((bf16[1,1,1,128,1024]{4,3,2,1,0:T(8,128)(2,1)S(1)}, bf16[1,1,1,128,1024]{4,3,2,1,0:T(8,128)(2,1)S(1)}, u32[]{:S(2)}, u32[]{:S(2)}) %collective-permute-start.46) | collective-permute-done | bytes 262176 | tf_op jit(solution)/shard_map/ppermute | solution.py:57
  135.4 3.4 collective-permute-start.25
  139.1 9.5 collective-permute-done.26
  155.5 4.3 collective-permute-start.40
  164.5 7.2 collective-permute-done.41
  182.9 37.5 %collective-permute-done.21 = bf16[4,1,1,64,2048]{4,3,2,1,0:T(8,128)(2,1)S(1)} collective-permute-done((bf16[4,1,1,64,2048]{4,3,2,1,0:T(8,128)(2,1)S(1)}, bf16[4,1,1,64,2048]{4,3,2,1,0:T(8,128)(2,1)S(1)}, u32[]{:S(2)}, u32[]{:S(2)}) %collective-permute-start.21) | collective-permute-done | bytes 1048608 | tf_op jit(solution)/shard_map/ppermute | solution.py:57
  225.4 59.4 %collective-permute-done.34 = bf16[4,1,1,64,2048]{4,3,2,1,0:T(8,128)(2,1)S(1)} collective-permute-done((bf16[4,1,1,64,2048]{4,3,2,1,0:T(8,128)(2,1)S(1)}, bf16[4,1,1,64,2048]{4,3,2,1,0:T(8,128)(2,1)S(1)}, u32[]{:S(2)}, u32[]{:S(2)}) %collective-permute-start.34) | collective-permute-done | bytes 1048608 | tf_op jit(solution)/shard_map/ppermute | solution.py:57
  316.1 4.7 maximum_select_fusion.1
  327.7 4.3 maximum_select_fusion.2
  332.1 3.6 multiply_convert_fusion.3
  346.6 22.8 %collective-permute-done.35 = bf16[4,1,2,64,2048]{4,3,2,1,0:T(8,128)(2,1)S(1)} collective-permute-done((bf16[4,1,2,64,2048]{4,3,2,1,0:T(8,128)(2,1)S(1)}, bf16[4,1,2,64,2048]{4,3,2,1,0:T(8,128)(2,1)S(1)}, u32[]{:S(2)}, u32[]{:S(2)}) %collective-permute-start.35) | collective-permute-done | bytes 2097184 | tf_op jit(solution)/shard_map/ppermute | solution.py:57
  402.5 5.8 maximum_select_fusion.4
  408.3 4.3 maximum_select_fusion.11
  419.0 4.4 maximum_select_fusion.5
  423.5 3.7 multiply_convert_fusion.2
  433.1 5.2 collective-permute-done.56
  438.3 3.6 collective-permute-done.55
  455.0 4.9 collective-permute-done.62
  524.8 4.8 collective-permute-done.72
  543.7 3.8 fusion.7
  585.0 3.5 multiply_convert_fusion.1
  603.5 3.4 fusion.14
  618.6 4.2 convert_add_fusion.3
  628.1 4.3 fusion.13
  643.8 47.1 %collective-permute-done.105 = bf16[4,1,1,64,2048]{4,3,2,1,0:T(8,128)(2,1)} collective-permute-done((bf16[4,1,1,64,2048]{4,3,2,1,0:T(8,128)(2,1)S(1)}, bf16[4,1,1,64,2048]{4,3,2,1,0:T(8,128)(2,1)}, u32[]{:S(2)}, u32[]{:S(2)}) %collective-permute-start.105) | collective-permute-done | bytes 1048608 | tf_op jit(solution)/shard_map/ppermute | solution.py:86
  705.1 5.4 collective-permute-done.127
  720.4 20.4 %collective-permute-done.119 = bf16[1,1,1,128,1024]{4,3,2,1,0:T(8,128)(2,1)S(1)} collective-permute-done((bf16[1,1,1,128,1024]{4,3,2,1,0:T(8,128)(2,1)S(1)}, bf16[1,1,1,128,1024]{4,3,2,1,0:T(8,128)(2,1)S(1)}, u32[]{:S(2)}, u32[]{:S(2)}) %collective-permute-start.119) | collective-permute-done | bytes 262176 | tf_op jit(solution)/shard_map/ppermute | solution.py:86
  751.3 3.5 convert_add_fusion
  778.6 3.4 fusion.18
  787.3 5.8 pad_maximum_fusion.1
  793.1 4.0 dynamic-slice_convert_fusion.5
  800.7 4.0 convert_add_fusion.4
  821.1 12.3 %collective-permute-done.94 = bf16[1,1,1,64,2192]{4,3,2,1,0:T(8,128)(2,1)S(1)} collective-permute-done((bf16[1,1,1,64,2192]{4,3,2,1,0:T(8,128)(2,1)S(1)}, bf16[1,1,1,64,2192]{4,3,2,1,0:T(8,128)(2,1)S(1)}, u32[]{:S(2)}, u32[]{:S(2)}) %collective-permute-start.94) | collective-permute-done | bytes 280608 | tf_op jit(solution)/shard_map/ppermute | solution.py:86
  839.5 28.6 %collective-permute-done.100 = bf16[4,1,1,64,2048]{4,3,2,1,0:T(8,128)(2,1)} collective-permute-done((bf16[4,1,1,64,2048]{4,3,2,1,0:T(8,128)(2,1)S(1)}, bf16[4,1,1,64,2048]{4,3,2,1,0:T(8,128)(2,1)}, u32[]{:S(2)}, u32[]{:S(2)}) %collective-permute-start.100) | collective-permute-done | bytes 1048608 | tf_op jit(solution)/shard_map/ppermute | solution.py:86
  870.3 3.6 convert_add_fusion.5
  882.0 6.8 collective-permute-done.101
  891.8 6.5 collective-permute-done.103
  899.3 11.5 %collective-permute-done.102 = bf16[1,1,1,64,2048]{4,3,2,1,0:T(8,128)(2,1)S(1)} collective-permute-done((bf16[1,1,1,64,2048]{4,3,2,1,0:T(8,128)(2,1)S(1)}, bf16[1,1,1,64,2048]{4,3,2,1,0:T(8,128)(2,1)S(1)}, u32[]{:S(2)}, u32[]{:S(2)}) %collective-permute-start.102) | collective-permute-done | bytes 262176 | tf_op jit(solution)/shard_map/ppermute | solution.py:86
  910.8 3.4 collective-permute-start.114
  915.8 5.0 collective-permute-done.115
  929.7 4.3 collective-permute-done.86
  933.9 13.6 %collective-permute-done.88 = bf16[1,1,1,64,2048]{4,3,2,1,0:T(8,128)(2,1)S(1)} collective-permute-done((bf16[1,1,1,64,2048]{4,3,2,1,0:T(8,128)(2,1)S(1)}, bf16[1,1,1,64,2048]{4,3,2,1,0:T(8,128)(2,1)S(1)}, u32[]{:S(2)}, u32[]{:S(2)}) %collective-permute-start.88) | collective-permute-done | bytes 262176 | tf_op jit(solution)/shard_map/ppermute | solution.py:86
  947.6 4.0 collective-permute-done.87
  (978 shorter events, 475.1 us)
Async XLA Ops:
  9.6 27.4 %collective-permute-start.1 = (bf16[64,2048]{1,0:T(8,128)(2,1)}, bf16[64,2048]{1,0:T(8,128)(2,1)}, u32[]{:S(2)}, u32[]{:S(2)}) collective-permute-start(bf16[64,2048]{1,0:T(8,128)(2,1)} %select_bitcast_fusion.3), channel_id=1, source_target_pairs={{0,16},{16,0},{1,17},{17,1},{2,18},{18,2},{3,19},{19,3},{4,20},{20... | collective-permute-start | bytes 786440 | tf_op jit(solution)/shard_map/ppermute | solution.py:92
  38.7 34.8 %collective-permute-start.3 = (bf16[1,1,1,64,2048]{4,3,2,1,0:T(8,128)(2,1)S(1)}, bf16[1,1,1,64,2048]{4,3,2,1,0:T(8,128)(2,1)S(1)}, u32[]{:S(2)}, u32[]{:S(2)}) collective-permute-start(bf16[1,1,1,64,2048]{4,3,2,1,0:T(8,128)(2,1)S(1)} %get-tuple-element.119), channel_id=1, source_target_pairs={{0,8},{1,9},{2,10},{3,11},{4,12},{5,13},{6,14},{7,15},{8,0},{9,1},... | collective-permute-start | bytes 786440 | tf_op jit(solution)/shard_map/ppermute | solution.py:57
  41.3 33.7 %collective-permute-start.2 = (bf16[1,1,1,64,2048]{4,3,2,1,0:T(8,128)(2,1)S(1)}, bf16[1,1,1,64,2048]{4,3,2,1,0:T(8,128)(2,1)S(1)}, u32[]{:S(2)}, u32[]{:S(2)}) collective-permute-start(bf16[1,1,1,64,2048]{4,3,2,1,0:T(8,128)(2,1)S(1)} %get-tuple-element.119), channel_id=1, source_target_pairs={{0,4},{1,5},{2,6},{3,7},{4,0},{5,1},{6,2},{7,3},{8,12},{9,13},{10,... | collective-permute-start | bytes 786440 | tf_op jit(solution)/shard_map/ppermute | solution.py:57
  41.7 56.3 %collective-permute-start.20 = (bf16[1,1,1,64,2048]{4,3,2,1,0:T(8,128)(2,1)S(1)}, bf16[1,1,1,64,2048]{4,3,2,1,0:T(8,128)(2,1)S(1)}, u32[]{:S(2)}, u32[]{:S(2)}) collective-permute-start(bf16[1,1,1,64,2048]{4,3,2,1,0:T(8,128)(2,1)S(1)} %get-tuple-element.133), channel_id=1, source_target_pairs={{0,12},{1,13},{2,14},{3,15},{4,8},{5,9},{6,10},{7,11},{8,4},{9,5},... | collective-permute-start | bytes 786440 | tf_op jit(solution)/shard_map/ppermute | solution.py:57
  43.0 58.6 %collective-permute-start.19 = (bf16[1,1,1,64,2048]{4,3,2,1,0:T(8,128)(2,1)S(1)}, bf16[1,1,1,64,2048]{4,3,2,1,0:T(8,128)(2,1)S(1)}, u32[]{:S(2)}, u32[]{:S(2)}) collective-permute-start(bf16[1,1,1,64,2048]{4,3,2,1,0:T(8,128)(2,1)S(1)} %get-tuple-element.133), channel_id=1, source_target_pairs={{0,8},{1,9},{2,10},{3,11},{4,12},{5,13},{6,14},{7,15},{8,0},{9,1},... | collective-permute-start | bytes 786440 | tf_op jit(solution)/shard_map/ppermute | solution.py:57
  58.6 46.4 %collective-permute-start.18 = (bf16[1,1,1,64,2048]{4,3,2,1,0:T(8,128)(2,1)S(1)}, bf16[1,1,1,64,2048]{4,3,2,1,0:T(8,128)(2,1)S(1)}, u32[]{:S(2)}, u32[]{:S(2)}) collective-permute-start(bf16[1,1,1,64,2048]{4,3,2,1,0:T(8,128)(2,1)S(1)} %get-tuple-element.133), channel_id=1, source_target_pairs={{0,4},{1,5},{2,6},{3,7},{4,0},{5,1},{6,2},{7,3},{8,12},{9,13},{10,... | collective-permute-start | bytes 786440 | tf_op jit(solution)/shard_map/ppermute | solution.py:57
  73.6 81.9 %collective-permute-start.33 = (bf16[1,1,1,64,2048]{4,3,2,1,0:T(8,128)(2,1)S(1)}, bf16[1,1,1,64,2048]{4,3,2,1,0:T(8,128)(2,1)S(1)}, u32[]{:S(2)}, u32[]{:S(2)}) collective-permute-start(bf16[1,1,1,64,2048]{4,3,2,1,0:T(8,128)(2,1)S(1)} %get-tuple-element.120), channel_id=1, source_target_pairs={{0,12},{1,13},{2,14},{3,15},{4,8},{5,9},{6,10},{7,11},{8,4},{9,5},... | collective-permute-start | bytes 786440 | tf_op jit(solution)/shard_map/ppermute | solution.py:57
  75.1 84.8 %collective-permute-start.32 = (bf16[1,1,1,64,2048]{4,3,2,1,0:T(8,128)(2,1)S(1)}, bf16[1,1,1,64,2048]{4,3,2,1,0:T(8,128)(2,1)S(1)}, u32[]{:S(2)}, u32[]{:S(2)}) collective-permute-start(bf16[1,1,1,64,2048]{4,3,2,1,0:T(8,128)(2,1)S(1)} %get-tuple-element.120), channel_id=1, source_target_pairs={{0,8},{1,9},{2,10},{3,11},{4,12},{5,13},{6,14},{7,15},{8,0},{9,1},... | collective-permute-start | bytes 786440 | tf_op jit(solution)/shard_map/ppermute | solution.py:57
  98.0 33.7 %collective-permute-start.46 = (bf16[1,1,1,128,1024]{4,3,2,1,0:T(8,128)(2,1)S(1)}, bf16[1,1,1,128,1024]{4,3,2,1,0:T(8,128)(2,1)S(1)}, u32[]{:S(2)}, u32[]{:S(2)}) collective-permute-start(bf16[1,1,1,128,1024]{4,3,2,1,0:T(8,128)(2,1)S(1)} %get-tuple-element.117), channel_id=1, source_target_pairs={{0,12},{1,13},{2,14},{3,15},{4,8},{5,9},{6,10},{7,11},{8,4},{9,5},... | collective-permute-start | bytes 786440 | tf_op jit(solution)/shard_map/ppermute | solution.py:57
  101.7 33.7 %collective-permute-start.45 = (bf16[1,1,1,128,1024]{4,3,2,1,0:T(8,128)(2,1)S(1)}, bf16[1,1,1,128,1024]{4,3,2,1,0:T(8,128)(2,1)S(1)}, u32[]{:S(2)}, u32[]{:S(2)}) collective-permute-start(bf16[1,1,1,128,1024]{4,3,2,1,0:T(8,128)(2,1)S(1)} %get-tuple-element.117), channel_id=1, source_target_pairs={{0,8},{1,9},{2,10},{3,11},{4,12},{5,13},{6,14},{7,15},{8,0},{9,1},... | collective-permute-start | bytes 786440 | tf_op jit(solution)/shard_map/ppermute | solution.py:57
  105.0 33.7 %collective-permute-start.44 = (bf16[1,1,1,128,1024]{4,3,2,1,0:T(8,128)(2,1)S(1)}, bf16[1,1,1,128,1024]{4,3,2,1,0:T(8,128)(2,1)S(1)}, u32[]{:S(2)}, u32[]{:S(2)}) collective-permute-start(bf16[1,1,1,128,1024]{4,3,2,1,0:T(8,128)(2,1)S(1)} %get-tuple-element.117), channel_id=1, source_target_pairs={{0,4},{1,5},{2,6},{3,7},{4,0},{5,1},{6,2},{7,3},{8,12},{9,13},{10,... | collective-permute-start | bytes 786440 | tf_op jit(solution)/shard_map/ppermute | solution.py:57
  152.4 26.1 %collective-permute-start.5 = (bf16[4,1,1,64,2048]{4,3,2,1,0:T(8,128)(2,1)S(1)}, bf16[4,1,1,64,2048]{4,3,2,1,0:T(8,128)(2,1)S(1)}, u32[]{:S(2)}, u32[]{:S(2)}) collective-permute-start(bf16[4,1,1,64,2048]{4,3,2,1,0:T(8,128)(2,1)S(1)} %pad_maximum_fusion.5), channel_id=1, source_target_pairs={{0,2},{1,3},{2,0},{3,1},{4,6},{5,7},{6,4},{7,5},{8,10},{9,11},{10,... | collective-permute-start | bytes 3145736 | tf_op jit(solution)/shard_map/ppermute | solution.py:57
  162.8 60.6 %collective-permute-start.27 = (bf16[4,1,1,128,1024]{4,3,2,1,0:T(8,128)(2,1)S(1)}, bf16[4,1,1,128,1024]{4,3,2,1,0:T(8,128)(2,1)S(1)}, u32[]{:S(2)}, u32[]{:S(2)}) collective-permute-start(bf16[4,1,1,128,1024]{4,3,2,1,0:T(8,128)(2,1)S(1)} %pad_maximum_fusion.9), channel_id=1, source_target_pairs={{0,2},{1,3},{2,0},{3,1},{4,6},{5,7},{6,4},{7,5},{8,10},{9,11},{10,... | collective-permute-start | bytes 3145736 | tf_op jit(solution)/shard_map/ppermute | solution.py:57
  171.7 170.1 %collective-permute-start.47 = (bf16[4,1,1,128,1024]{4,3,2,1,0:T(8,128)(2,1)}, bf16[4,1,1,128,1024]{4,3,2,1,0:T(8,128)(2,1)}, u32[]{:S(2)}, u32[]{:S(2)}) collective-permute-start(bf16[4,1,1,128,1024]{4,3,2,1,0:T(8,128)(2,1)} %pad_maximum_fusion.15), channel_id=1, source_target_pairs={{0,1},{1,0},{2,3},{3,2},{4,5},{5,4},{6,7},{7,6},{8,9},{9,8},{10,11... | collective-permute-start | bytes 3145736 | tf_op jit(solution)/shard_map/ppermute | solution.py:57
  173.7 46.8 %collective-permute-start.21 = (bf16[4,1,1,64,2048]{4,3,2,1,0:T(8,128)(2,1)S(1)}, bf16[4,1,1,64,2048]{4,3,2,1,0:T(8,128)(2,1)S(1)}, u32[]{:S(2)}, u32[]{:S(2)}) collective-permute-start(bf16[4,1,1,64,2048]{4,3,2,1,0:T(8,128)(2,1)S(1)} %pad_maximum_fusion.7), channel_id=1, source_target_pairs={{0,1},{1,0},{2,3},{3,2},{4,5},{5,4},{6,7},{7,6},{8,9},{9,8},{10,11... | collective-permute-start | bytes 3145736 | tf_op jit(solution)/shard_map/ppermute | solution.py:57
  179.0 108.4 %collective-permute-start.6 = (bf16[4,2,1,64,2048]{4,3,2,1,0:T(8,128)(2,1)S(1)}, bf16[4,2,1,64,2048]{4,3,2,1,0:T(8,128)(2,1)S(1)}, u32[]{:S(2)}, u32[]{:S(2)}) collective-permute-start(bf16[4,2,1,64,2048]{4,3,2,1,0:T(8,128)(2,1)S(1)} %maximum_select_fusion.6), channel_id=1, source_target_pairs={{0,1},{1,0},{2,3},{3,2},{4,5},{5,4},{6,7},{7,6},{8,9},{9,8},{10,11... | collective-permute-start | bytes 6291464 | tf_op jit(solution)/shard_map/ppermute | solution.py:57
  181.7 103.1 %collective-permute-start.34 = (bf16[4,1,1,64,2048]{4,3,2,1,0:T(8,128)(2,1)S(1)}, bf16[4,1,1,64,2048]{4,3,2,1,0:T(8,128)(2,1)S(1)}, u32[]{:S(2)}, u32[]{:S(2)}) collective-permute-start(bf16[4,1,1,64,2048]{4,3,2,1,0:T(8,128)(2,1)S(1)} %pad_maximum_fusion.11), channel_id=1, source_target_pairs={{0,1},{1,0},{2,3},{3,2},{4,5},{5,4},{6,7},{7,6},{8,9},{9,8},{10,11... | collective-permute-start | bytes 3145736 | tf_op jit(solution)/shard_map/ppermute | solution.py:57
  220.5 117.8 %collective-permute-start.42 = (bf16[4,1,1,64,2048]{4,3,2,1,0:T(8,128)(2,1)}, bf16[4,1,1,64,2048]{4,3,2,1,0:T(8,128)(2,1)}, u32[]{:S(2)}, u32[]{:S(2)}) collective-permute-start(bf16[4,1,1,64,2048]{4,3,2,1,0:T(8,128)(2,1)} %pad_maximum_fusion.13), channel_id=1, source_target_pairs={{0,2},{1,3},{2,0},{3,1},{4,6},{5,7},{6,4},{7,5},{8,10},{9,11},{10,... | collective-permute-start | bytes 3145736 | tf_op jit(solution)/shard_map/ppermute | solution.py:57
  223.5 92.1 %collective-permute-start.22 = (bf16[4,1,2,64,2048]{4,3,2,1,0:T(8,128)(2,1)}, bf16[4,1,2,64,2048]{4,3,2,1,0:T(8,128)(2,1)}, u32[]{:S(2)}, u32[]{:S(2)}) collective-permute-start(bf16[4,1,2,64,2048]{4,3,2,1,0:T(8,128)(2,1)} %maximum_select_fusion.8), channel_id=1, source_target_pairs={{0,2},{1,3},{2,0},{3,1},{4,6},{5,7},{6,4},{7,5},{8,10},{9,11},{10,... | collective-permute-start | bytes 6291464 | tf_op jit(solution)/shard_map/ppermute | solution.py:57
  284.8 42.9 %collective-permute-start.28 = (bf16[4,2,1,128,1024]{4,3,2,1,0:T(8,128)(2,1)}, bf16[4,2,1,128,1024]{4,3,2,1,0:T(8,128)(2,1)}, u32[]{:S(2)}, u32[]{:S(2)}) collective-permute-start(bf16[4,2,1,128,1024]{4,3,2,1,0:T(8,128)(2,1)} %maximum_select_fusion.9), channel_id=1, source_target_pairs={{0,1},{1,0},{2,3},{3,2},{4,5},{5,4},{6,7},{7,6},{8,9},{9,8},{10,11... | collective-permute-start | bytes 6291464 | tf_op jit(solution)/shard_map/ppermute | solution.py:57
  289.2 33.5 %collective-permute-start.8 = (bf16[1024,512]{1,0:T(8,128)(2,1)}, bf16[1024,512]{1,0:T(8,128)(2,1)}, u32[]{:S(2)}, u32[]{:S(2)}) collective-permute-start(bf16[1024,512]{1,0:T(8,128)(2,1)} %slice.470), channel_id=1, source_target_pairs={{0,16},{16,0},{1,17},{17,1},{2,18},{18,2},{3,19},{19,3},{4,20},{20... | collective-permute-start | bytes 3145736 | tf_op jit(solution)/shard_map/ppermute | solution.py:92
  320.8 48.6 %collective-permute-start.35 = (bf16[4,1,2,64,2048]{4,3,2,1,0:T(8,128)(2,1)S(1)}, bf16[4,1,2,64,2048]{4,3,2,1,0:T(8,128)(2,1)S(1)}, u32[]{:S(2)}, u32[]{:S(2)}) collective-permute-start(bf16[4,1,2,64,2048]{4,3,2,1,0:T(8,128)(2,1)S(1)} %copy-done.13), channel_id=1, source_target_pairs={{0,2},{1,3},{2,0},{3,1},{4,6},{5,7},{6,4},{7,5},{8,10},{9,11},{10,... | collective-permute-start | bytes 6291464 | tf_op jit(solution)/shard_map/ppermute | solution.py:57
  340.9 61.6 %collective-permute-start.43 = (bf16[4,2,1,64,2048]{4,3,2,1,0:T(8,128)(2,1)}, bf16[4,2,1,64,2048]{4,3,2,1,0:T(8,128)(2,1)}, u32[]{:S(2)}, u32[]{:S(2)}) collective-permute-start(bf16[4,2,1,64,2048]{4,3,2,1,0:T(8,128)(2,1)} %maximum_select_fusion.12), channel_id=1, source_target_pairs={{0,1},{1,0},{2,3},{3,2},{4,5},{5,4},{6,7},{7,6},{8,9},{9,8},{10,11... | collective-permute-start | bytes 6291464 | tf_op jit(solution)/shard_map/ppermute | solution.py:57
  344.5 74.5 %collective-permute-start.48 = (bf16[4,1,2,128,1024]{4,3,2,1,0:T(8,128)(2,1)}, bf16[4,1,2,128,1024]{4,3,2,1,0:T(8,128)(2,1)}, u32[]{:S(2)}, u32[]{:S(2)}) collective-permute-start(bf16[4,1,2,128,1024]{4,3,2,1,0:T(8,128)(2,1)} %maximum_select_fusion.13), channel_id=1, source_target_pairs={{0,2},{1,3},{2,0},{3,1},{4,6},{5,7},{6,4},{7,5},{8,10},{9,11},{10,... | collective-permute-start | bytes 6291464 | tf_op jit(solution)/shard_map/ppermute | solution.py:57
  371.3 37.1 %collective-permute-start.37 = (bf16[1024,512]{1,0:T(8,128)(2,1)}, bf16[1024,512]{1,0:T(8,128)(2,1)}, u32[]{:S(2)}, u32[]{:S(2)}) collective-permute-start(bf16[1024,512]{1,0:T(8,128)(2,1)} %slice.492), channel_id=1, source_target_pairs={{0,16},{16,0},{1,17},{17,1},{2,18},{18,2},{3,19},{19,3},{4,20},{20... | collective-permute-start | bytes 3145736 | tf_op jit(solution)/shard_map/ppermute | solution.py:92
  506.4 30.1 %collective-permute-start.69 = (f32[1]{0:T(128)}, f32[1]{0:T(128)}, u32[]{:S(2)}, u32[]{:S(2)}) collective-permute-start(f32[1]{0:T(128)} %bitcast.68), channel_id=1, source_target_pairs={{0,16},{16,0},{1,17},{17,1},{2,18},{18,2},{3,19},{19,3},{4,20},{20... | collective-permute-start | bytes 20 | tf_op jit(solution)/shard_map/ppermute | solution.py:92
  555.9 62.7 %collective-permute-start.104 = (bf16[4,2,1,64,2048]{4,3,2,1,0:T(8,128)(2,1)}, bf16[4,2,1,64,2048]{4,3,2,1,0:T(8,128)(2,1)}, u32[]{:S(2)}, u32[]{:S(2)}) collective-permute-start(bf16[4,2,1,64,2048]{4,3,2,1,0:T(8,128)(2,1)} %dynamic-slice_convert_fusion.3), channel_id=1, source_target_pairs={{0,1},{1,0},{2,3},{3,2},{4,5},{5,4},{6,7},{7,6},{8,9},{9,8},{10,11... | collective-permute-start | bytes 6291464 | tf_op jit(solution)/shard_map/ppermute | solution.py:86
  563.7 59.9 %collective-permute-start.116 = (bf16[4,1,2,128,1024]{4,3,2,1,0:T(8,128)(2,1)}, bf16[4,1,2,128,1024]{4,3,2,1,0:T(8,128)(2,1)}, u32[]{:S(2)}, u32[]{:S(2)}) collective-permute-start(bf16[4,1,2,128,1024]{4,3,2,1,0:T(8,128)(2,1)} %dynamic-slice_convert_fusion.1), channel_id=1, source_target_pairs={{0,2},{1,3},{2,0},{3,1},{4,6},{5,7},{6,4},{7,5},{8,10},{9,11},{10,... | collective-permute-start | bytes 6291464 | tf_op jit(solution)/shard_map/ppermute | solution.py:86
  614.8 136.5 %collective-permute-start.90 = (bf16[4,1,2,64,2192]{4,3,2,1,0:T(8,128)(2,1)}, bf16[4,1,2,64,2192]{4,3,2,1,0:T(8,128)(2,1)}, u32[]{:S(2)}, u32[]{:S(2)}) collective-permute-start(bf16[4,1,2,64,2192]{4,3,2,1,0:T(8,128)(2,1)} %dynamic-slice_convert_fusion), channel_id=1, source_target_pairs={{0,2},{1,3},{2,0},{3,1},{4,6},{5,7},{6,4},{7,5},{8,10},{9,11},{10,... | collective-permute-start | bytes 6733832 | tf_op jit(solution)/shard_map/ppermute | solution.py:86
  623.0 67.9 %collective-permute-start.105 = (bf16[4,1,1,64,2048]{4,3,2,1,0:T(8,128)(2,1)S(1)}, bf16[4,1,1,64,2048]{4,3,2,1,0:T(8,128)(2,1)}, u32[]{:S(2)}, u32[]{:S(2)}) collective-permute-start(bf16[4,1,1,64,2048]{4,3,2,1,0:T(8,128)(2,1)S(1)} %dynamic-slice_convert_fusion.9), channel_id=1, source_target_pairs={{0,2},{1,3},{2,0},{3,1},{4,6},{5,7},{6,4},{7,5},{8,10},{9,11},{10,... | collective-permute-start | bytes 3145736 | tf_op jit(solution)/shard_map/ppermute | solution.py:86
  626.9 65.7 %collective-permute-start.117 = (bf16[4,1,1,128,1024]{4,3,2,1,0:T(8,128)(2,1)S(1)}, bf16[4,1,1,128,1024]{4,3,2,1,0:T(8,128)(2,1)S(1)}, u32[]{:S(2)}, u32[]{:S(2)}) collective-permute-start(bf16[4,1,1,128,1024]{4,3,2,1,0:T(8,128)(2,1)S(1)} %dynamic-slice_convert_fusion.7), channel_id=1, source_target_pairs={{0,1},{1,0},{2,3},{3,2},{4,5},{5,4},{6,7},{7,6},{8,9},{9,8},{10,11... | collective-permute-start | bytes 3145736 | tf_op jit(solution)/shard_map/ppermute | solution.py:86
  634.3 59.5 %collective-permute-start.81 = (f32[192,1024]{1,0:T(8,128)S(1)}, f32[192,1024]{1,0:T(8,128)S(1)}, u32[]{:S(2)}, u32[]{:S(2)}) collective-permute-start(f32[192,1024]{1,0:T(8,128)S(1)} %slice.525), channel_id=1, source_target_pairs={{0,16},{16,0},{1,17},{17,1},{2,18},{18,2},{3,19},{19,3},{4,20},{20... | collective-permute-start | bytes 2359304 | tf_op jit(solution)/shard_map/ppermute | solution.py:92
  714.9 28.5 %collective-permute-start.106 = (bf16[1,1,1,64,2048]{4,3,2,1,0:T(8,128)(2,1)S(1)}, bf16[1,1,1,64,2048]{4,3,2,1,0:T(8,128)(2,1)S(1)}, u32[]{:S(2)}, u32[]{:S(2)}) collective-permute-start(bf16[1,1,1,64,2048]{4,3,2,1,0:T(8,128)(2,1)S(1)} %get-tuple-element.62), channel_id=1, source_target_pairs={{0,4},{1,5},{2,6},{3,7},{4,0},{5,1},{6,2},{7,3},{8,12},{9,13},{10,... | collective-permute-start | bytes 786440 | tf_op jit(solution)/shard_map/ppermute | solution.py:86
  714.9 25.8 %collective-permute-start.119 = (bf16[1,1,1,128,1024]{4,3,2,1,0:T(8,128)(2,1)S(1)}, bf16[1,1,1,128,1024]{4,3,2,1,0:T(8,128)(2,1)S(1)}, u32[]{:S(2)}, u32[]{:S(2)}) collective-permute-start(bf16[1,1,1,128,1024]{4,3,2,1,0:T(8,128)(2,1)S(1)} %get-tuple-element.58), channel_id=1, source_target_pairs={{0,8},{1,9},{2,10},{3,11},{4,12},{5,13},{6,14},{7,15},{8,0},{9,1},... | collective-permute-start | bytes 786440 | tf_op jit(solution)/shard_map/ppermute | solution.py:86
  717.4 30.5 %collective-permute-start.108 = (bf16[1,1,1,64,2048]{4,3,2,1,0:T(8,128)(2,1)S(1)}, bf16[1,1,1,64,2048]{4,3,2,1,0:T(8,128)(2,1)S(1)}, u32[]{:S(2)}, u32[]{:S(2)}) collective-permute-start(bf16[1,1,1,64,2048]{4,3,2,1,0:T(8,128)(2,1)S(1)} %get-tuple-element.63), channel_id=1, source_target_pairs={{0,12},{1,13},{2,14},{3,15},{4,8},{5,9},{6,10},{7,11},{8,4},{9,5},... | collective-permute-start | bytes 786440 | tf_op jit(solution)/shard_map/ppermute | solution.py:86
  718.5 30.9 %collective-permute-start.107 = (bf16[1,1,1,64,2048]{4,3,2,1,0:T(8,128)(2,1)S(1)}, bf16[1,1,1,64,2048]{4,3,2,1,0:T(8,128)(2,1)S(1)}, u32[]{:S(2)}, u32[]{:S(2)}) collective-permute-start(bf16[1,1,1,64,2048]{4,3,2,1,0:T(8,128)(2,1)S(1)} %get-tuple-element.64), channel_id=1, source_target_pairs={{0,8},{1,9},{2,10},{3,11},{4,12},{5,13},{6,14},{7,15},{8,0},{9,1},... | collective-permute-start | bytes 786440 | tf_op jit(solution)/shard_map/ppermute | solution.py:86
  740.8 59.9 %collective-permute-start.99 = (bf16[4,1,2,64,2048]{4,3,2,1,0:T(8,128)(2,1)}, bf16[4,1,2,64,2048]{4,3,2,1,0:T(8,128)(2,1)}, u32[]{:S(2)}, u32[]{:S(2)}) collective-permute-start(bf16[4,1,2,64,2048]{4,3,2,1,0:T(8,128)(2,1)} %dynamic-slice_convert_fusion.4), channel_id=1, source_target_pairs={{0,2},{1,3},{2,0},{3,1},{4,6},{5,7},{6,4},{7,5},{8,10},{9,11},{10,... | collective-permute-start | bytes 6291464 | tf_op jit(solution)/shard_map/ppermute | solution.py:86
  743.4 68.4 %collective-permute-start.111 = (bf16[4,2,1,128,1024]{4,3,2,1,0:T(8,128)(2,1)}, bf16[4,2,1,128,1024]{4,3,2,1,0:T(8,128)(2,1)}, u32[]{:S(2)}, u32[]{:S(2)}) collective-permute-start(bf16[4,2,1,128,1024]{4,3,2,1,0:T(8,128)(2,1)} %dynamic-slice_convert_fusion.2), channel_id=1, source_target_pairs={{0,1},{1,0},{2,3},{3,2},{4,5},{5,4},{6,7},{7,6},{8,9},{9,8},{10,11... | collective-permute-start | bytes 6291464 | tf_op jit(solution)/shard_map/ppermute | solution.py:86
  758.1 47.9 %collective-permute-start.91 = (bf16[4,1,1,64,2192]{4,3,2,1,0:T(8,128)(2,1)}, bf16[4,1,1,64,2192]{4,3,2,1,0:T(8,128)(2,1)}, u32[]{:S(2)}, u32[]{:S(2)}) collective-permute-start(bf16[4,1,1,64,2192]{4,3,2,1,0:T(8,128)(2,1)} %dynamic-slice_convert_fusion.6), channel_id=1, source_target_pairs={{0,1},{1,0},{2,3},{3,2},{4,5},{5,4},{6,7},{7,6},{8,9},{9,8},{10,11... | collective-permute-start | bytes 3366920 | tf_op jit(solution)/shard_map/ppermute | solution.py:86
  797.1 73.2 %collective-permute-start.84 = (bf16[4,2,1,64,2048]{4,3,2,1,0:T(8,128)(2,1)}, bf16[4,2,1,64,2048]{4,3,2,1,0:T(8,128)(2,1)}, u32[]{:S(2)}, u32[]{:S(2)}) collective-permute-start(bf16[4,2,1,64,2048]{4,3,2,1,0:T(8,128)(2,1)} %dynamic-slice_convert_fusion.5), channel_id=1, source_target_pairs={{0,1},{1,0},{2,3},{3,2},{4,5},{5,4},{6,7},{7,6},{8,9},{9,8},{10,11... | collective-permute-start | bytes 6291464 | tf_op jit(solution)/shard_map/ppermute | solution.py:86
  805.1 63.0 %collective-permute-start.100 = (bf16[4,1,1,64,2048]{4,3,2,1,0:T(8,128)(2,1)S(1)}, bf16[4,1,1,64,2048]{4,3,2,1,0:T(8,128)(2,1)}, u32[]{:S(2)}, u32[]{:S(2)}) collective-permute-start(bf16[4,1,1,64,2048]{4,3,2,1,0:T(8,128)(2,1)S(1)} %dynamic-slice_convert_fusion.10), channel_id=1, source_target_pairs={{0,1},{1,0},{2,3},{3,2},{4,5},{5,4},{6,7},{7,6},{8,9},{9,8},{10,11... | collective-permute-start | bytes 3145736 | tf_op jit(solution)/shard_map/ppermute | solution.py:86
  819.0 58.8 %collective-permute-start.109 = (f32[64,2048]{1,0:T(8,128)S(1)}, f32[64,2048]{1,0:T(8,128)}, u32[]{:S(2)}, u32[]{:S(2)}) collective-permute-start(f32[64,2048]{1,0:T(8,128)S(1)} %copy-done.61), channel_id=1, source_target_pairs={{0,16},{1,17},{2,18},{3,19},{4,20},{5,21},{6,22},{7,23},{8,24},{9,... | collective-permute-start | bytes 1572872 | tf_op jit(solution)/shard_map/ppermute | solution.py:96
  833.4 81.0 %collective-permute-start.121 = (f32[128,1024]{1,0:T(8,128)S(1)}, f32[128,1024]{1,0:T(8,128)S(1)}, u32[]{:S(2)}, u32[]{:S(2)}) collective-permute-start(f32[128,1024]{1,0:T(8,128)S(1)} %copy-done.60), channel_id=1, source_target_pairs={{0,16},{1,17},{2,18},{3,19},{4,20},{5,21},{6,22},{7,23},{8,24},{9,... | collective-permute-start | bytes 1572872 | tf_op jit(solution)/shard_map/ppermute | solution.py:96
  836.5 42.3 %collective-permute-start.112 = (bf16[4,1,1,128,1024]{4,3,2,1,0:T(8,128)(2,1)}, bf16[4,1,1,128,1024]{4,3,2,1,0:T(8,128)(2,1)}, u32[]{:S(2)}, u32[]{:S(2)}) collective-permute-start(bf16[4,1,1,128,1024]{4,3,2,1,0:T(8,128)(2,1)} %dynamic-slice_convert_fusion.8), channel_id=1, source_target_pairs={{0,2},{1,3},{2,0},{3,1},{4,6},{5,7},{6,4},{7,5},{8,10},{9,11},{10,... | collective-permute-start | bytes 3145736 | tf_op jit(solution)/shard_map/ppermute | solution.py:86
  874.0 49.6 %collective-permute-start.85 = (bf16[4,1,1,64,2048]{4,3,2,1,0:T(8,128)(2,1)S(1)}, bf16[4,1,1,64,2048]{4,3,2,1,0:T(8,128)(2,1)S(1)}, u32[]{:S(2)}, u32[]{:S(2)}) collective-permute-start(bf16[4,1,1,64,2048]{4,3,2,1,0:T(8,128)(2,1)S(1)} %dynamic-slice_convert_fusion.11), channel_id=1, source_target_pairs={{0,2},{1,3},{2,0},{3,1},{4,6},{5,7},{6,4},{7,5},{8,10},{9,11},{10,... | collective-permute-start | bytes 3145736 | tf_op jit(solution)/shard_map/ppermute | solution.py:86
  878.8 32.0 %collective-permute-start.102 = (bf16[1,1,1,64,2048]{4,3,2,1,0:T(8,128)(2,1)S(1)}, bf16[1,1,1,64,2048]{4,3,2,1,0:T(8,128)(2,1)S(1)}, u32[]{:S(2)}, u32[]{:S(2)}) collective-permute-start(bf16[1,1,1,64,2048]{4,3,2,1,0:T(8,128)(2,1)S(1)} %get-tuple-element.61), channel_id=1, source_target_pairs={{0,8},{1,9},{2,10},{3,11},{4,12},{5,13},{6,14},{7,15},{8,0},{9,1},... | collective-permute-start | bytes 786440 | tf_op jit(solution)/shard_map/ppermute | solution.py:86
  888.8 27.0 %collective-permute-start.113 = (bf16[1,1,1,128,1024]{4,3,2,1,0:T(8,128)(2,1)S(1)}, bf16[1,1,1,128,1024]{4,3,2,1,0:T(8,128)(2,1)S(1)}, u32[]{:S(2)}, u32[]{:S(2)}) collective-permute-start(bf16[1,1,1,128,1024]{4,3,2,1,0:T(8,128)(2,1)S(1)} %get-tuple-element.53), channel_id=1, source_target_pairs={{0,4},{1,5},{2,6},{3,7},{4,0},{5,1},{6,2},{7,3},{8,12},{9,13},{10,... | collective-permute-start | bytes 786440 | tf_op jit(solution)/shard_map/ppermute | solution.py:86
  922.4 30.6 %collective-permute-start.122 = (f32[128,1024]{1,0:T(8,128)S(1)}, f32[128,1024]{1,0:T(8,128)S(1)}, u32[]{:S(2)}, u32[]{:S(2)}) collective-permute-start(f32[128,1024]{1,0:T(8,128)S(1)} %get-tuple-element.30), channel_id=1, source_target_pairs={{16,0},{17,1},{18,2},{19,3},{20,4},{21,5},{22,6},{23,7},{24,8},{25... | collective-permute-start | bytes 1572872 | tf_op jit(solution)/shard_map/ppermute | solution.py:96
  (262 other events, 4036.2 us)
